TPU v7x, 256 devices: a whole 4x4x8 slice. The times are simulated.
256 devices in a mesh: ctr: 8 (over x, core), comp: 32 (over y, z).
Axes of the slice: x: 4, y: 4, z: 8, core: 2. Of those that a mesh axis runs over, the one named last changes fastest.
Arguments:
- initial: float32 [64, 1024, 1024], P('ctr', 'comp'), may hold values from 0 to 2
- rates_first: float32 [1024, 1024], replicated, may hold values from 0.01 to 1
- blocks_first: int32 [16, 16], replicated, may hold values 0 or 1
- rates_second: float32 [1024, 1024], replicated, may hold values from 0.01 to 1
- blocks_second: int32 [16, 16], replicated, may hold values 0 or 1
- level_rate: float32 [64], replicated, may hold values from 30 to 300
- level_code: int32 [64], replicated, may hold values from 0 to 3
Outputs:
- transient: float32 [64, 1024, 1024], P('ctr', 'comp')
- stepped: float32 [64, 1024, 1024], P('ctr', 'comp')
All inputs are finite; a program needn't handle non-finite values.
Results may differ from a plain program's by a relative error of at most 0.000071.
Values sent between devices are 32-bit elements; how exact they have to be, the bound alone decides.
No kernel may reach another device: no remote copies, remote signals or barrier semaphores. Data moves between devices by JAX's collectives and lax.ppermute only.
A program may use at most 128 MiB of HBM per device.

v0:
```python
import functools

import jax
import jax.numpy as jnp
from jax import lax
from jax.experimental import pallas as pl
from jax.experimental.pallas import tpu as pltpu
from jax.sharding import PartitionSpec as P

F32 = jnp.float32
BF16 = jnp.bfloat16
LANES = 256
OFFSETS = (-2, -1, 1, 2)
WHOLE = pl.BlockSpec(memory_space=pltpu.VMEM)
SCALARS = pl.BlockSpec(memory_space=pltpu.SMEM)


def params(mib):
    return pltpu.CompilerParams(vmem_limit_bytes=mib << 20)


def halves(x):
    high = x.astype(BF16)
    return high, (x - high.astype(F32)).astype(BF16)


def mm(a, b):
    return jnp.dot(a, b, preferred_element_type=F32)


def masked_rows(rates_ref, blocks_ref):
    tall, order = rates_ref.shape
    nblk = blocks_ref.shape[0]
    width = order // nblk
    first = pl.program_id(0) * (tall // width)
    row = lax.broadcasted_iota(jnp.int32, (tall, nblk), 0) // width + first
    left = (row == lax.broadcasted_iota(jnp.int32, (tall, nblk), 1)).astype(BF16)
    col = lax.broadcasted_iota(jnp.int32, (nblk, order), 1) // width
    right = (col == lax.broadcasted_iota(jnp.int32, (nblk, order), 0)).astype(BF16)
    wide = mm(blocks_ref[...].astype(F32).astype(BF16), right).astype(BF16)
    return rates_ref[...] * mm(left, wide)


def expand_kernel(turn, rates_ref, blocks_ref, high_ref, low_ref, exits_ref):
    full = masked_rows(rates_ref, blocks_ref)
    exits_ref[...] = jnp.sum(full, axis=1, keepdims=True)
    high, low = halves(full.T if turn else full)
    high_ref[...] = high
    low_ref[...] = low


def expand(rates, blocks, turn, tall=256):
    order = rates.shape[0]
    rows = pl.BlockSpec((tall, order), lambda i: (i, 0))
    out = pl.BlockSpec((order, tall), lambda i: (0, i)) if turn else rows
    return pl.pallas_call(
        functools.partial(expand_kernel, turn),
        grid=(order // tall,),
        in_specs=[rows, pl.BlockSpec(blocks.shape, lambda i: (0, 0))],
        out_specs=[out, out, pl.BlockSpec((tall, 1), lambda i: (i, 0))],
        out_shape=[
            jax.ShapeDtypeStruct((order, order), BF16),
            jax.ShapeDtypeStruct((order, order), BF16),
            jax.ShapeDtypeStruct((order, 1), F32),
        ],
        compiler_params=params(16),
        cost_estimate=pl.CostEstimate(flops=1 << 26, bytes_accessed=8 << 20, transcendentals=0),
        name="expand_turned" if turn else "expand",
    )(rates, blocks)


def turned_kernel(high_ref, low_ref, exits_ref, scale_ref, mass_ref, out_ref):
    scale = scale_ref[0]
    order = high_ref.shape[0]
    high, low = halves(mass_ref[...])
    for at in range(0, order, 256):
        rows = pl.ds(at, 256)
        left = high_ref[rows, :]
        total = mm(left, high) + mm(left, low) + mm(low_ref[rows, :], high)
        out_ref[rows, :] = (total - mass_ref[rows, :] * exits_ref[rows, :]) * scale


def turned(high, low, exits, scale, mass):
    return pl.pallas_call(
        turned_kernel,
        in_specs=[WHOLE, WHOLE, WHOLE, SCALARS, WHOLE],
        out_specs=WHOLE,
        out_shape=jax.ShapeDtypeStruct(mass.shape, F32),
        compiler_params=params(20),
        cost_estimate=pl.CostEstimate(flops=3 << 29, bytes_accessed=6 << 20, transcendentals=0),
        name="second",
    )(high, low, exits, scale, mass)


def product(x, high_ref, low_ref, cols):
    high, low = x
    return mm(high, high_ref[:, cols]) + mm(low, high_ref[:, cols]) + mm(high, low_ref[:, cols])


def hops(coef_ref, m, get, levels):
    total = None
    for k, offset in enumerate(OFFSETS):
        source = get(m - offset)
        if source is not None:
            part = coef_ref[k, m] * source
            total = part if total is None else total + part
    return total


def first_kernel(high_ref, low_ref, exits_ref, coef_ref, v_ref, below_ref, above_ref, out_ref):
    levels, rows, order = v_ref.shape
    x = halves(v_ref[...].reshape(levels * rows, order))
    scale = coef_ref[5, 0]
    for at in range(0, order, 256):
        cols = pl.ds(at, 256)
        prod = product(x, high_ref, low_ref, cols).reshape(levels, rows, 256)

        def get(n, cols=cols):
            if n < 0:
                return below_ref[n + 2, :, cols]
            if n >= levels:
                return above_ref[n - levels, :, cols]
            return v_ref[n, :, cols]

        for m in range(levels):
            here = v_ref[m, :, cols]
            change = prod[m] - here * (exits_ref[:, cols] + coef_ref[4, m])
            out_ref[m, :, cols] = here + scale * (change + hops(coef_ref, m, get, levels))


def first(high, low, exits, coef, v, below, above):
    return pl.pallas_call(
        first_kernel,
        in_specs=[WHOLE, WHOLE, WHOLE, SCALARS, WHOLE, WHOLE, WHOLE],
        out_specs=WHOLE,
        out_shape=jax.ShapeDtypeStruct(v.shape, F32),
        compiler_params=params(20),
        cost_estimate=pl.CostEstimate(flops=3 << 29, bytes_accessed=7 << 20, transcendentals=0),
        name="first",
    )(high, low, exits, coef, v, below, above)


def gather_kernel(bv_ref, w_ref, sum_ref, low_ref, top_ref):
    levels, _, order = bv_ref.shape
    parts = order // LANES
    for m in range(levels):
        for p in range(parts):
            cols = pl.ds(p * LANES, LANES)
            s = bv_ref[m, :, cols] + 2.0 * w_ref[m * parts + p]
            sum_ref[m, :, cols] = s
            if m < 2:
                low_ref[m, :, cols] = s
            if m >= levels - 2:
                top_ref[m - levels + 2, :, cols] = s


def gather(bv, w):
    levels, rows, order = bv.shape
    edge = jax.ShapeDtypeStruct((2, rows, order), F32)
    return pl.pallas_call(
        gather_kernel,
        in_specs=[WHOLE, WHOLE],
        out_specs=[WHOLE, WHOLE, WHOLE],
        out_shape=[jax.ShapeDtypeStruct(bv.shape, F32), edge, edge],
        compiler_params=params(12),
        cost_estimate=pl.CostEstimate(flops=1 << 20, bytes_accessed=4 << 20, transcendentals=0),
        name="once",
    )(bv, w)


def twice_kernel(high_ref, low_ref, exits_ref, coef_ref, v_ref, bv_ref, s_ref, step_ref, trans_ref):
    levels, rows, order = v_ref.shape
    x = halves(s_ref[...].reshape(levels * rows, order))
    scale = coef_ref[5, 0]
    for at in range(0, order, 256):
        cols = pl.ds(at, 256)
        prod = product(x, high_ref, low_ref, cols).reshape(levels, rows, 256)

        def get(n, cols=cols):
            return s_ref[n, :, cols] if 0 <= n < levels else None

        for m in range(levels):
            here = s_ref[m, :, cols]
            change = prod[m] - here * (exits_ref[:, cols] + coef_ref[4, m])
            stepped = here + scale * (change + hops(coef_ref, m, get, levels))
            once = 0.5 * (here + bv_ref[m, :, cols])
            step_ref[m, :, cols] = stepped
            trans_ref[m, :, cols] = (v_ref[m, :, cols] + once) * 0.4 + 0.2 * stepped


def twice(high, low, exits, coef, v, bv, s):
    shape = jax.ShapeDtypeStruct(v.shape, F32)
    return pl.pallas_call(
        twice_kernel,
        in_specs=[WHOLE, WHOLE, WHOLE, SCALARS, WHOLE, WHOLE, WHOLE],
        out_specs=[WHOLE, WHOLE],
        out_shape=[shape, shape],
        compiler_params=params(24),
        cost_estimate=pl.CostEstimate(flops=3 << 29, bytes_accessed=9 << 20, transcendentals=0),
        name="twice",
    )(high, low, exits, coef, v, bv, s)


def finish_kernel(coef_ref, step_ref, trans_ref, below_ref, above_ref, w_ref, out_t_ref, out_s_ref):
    levels, _, order = step_ref.shape
    parts = order // LANES
    scale = coef_ref[5, 0]
    for m in range(levels):
        for p in range(parts):
            cols = pl.ds(p * LANES, LANES)

            def get(n, cols=cols):
                if n < 0:
                    return below_ref[n + 2, :, cols]
                return above_ref[n - levels, :, cols] if n >= levels else None

            more = w_ref[m * parts + p]
            far = hops(coef_ref, m, get, levels)
            if far is not None:
                more = more + scale * far
            out_s_ref[m, :, cols] = step_ref[m, :, cols] + more
            out_t_ref[m, :, cols] = trans_ref[m, :, cols] + 0.2 * more


def finish(coef, step, trans, below, above, w):
    shape = jax.ShapeDtypeStruct(step.shape, F32)
    return pl.pallas_call(
        finish_kernel,
        in_specs=[SCALARS, WHOLE, WHOLE, WHOLE, WHOLE, WHOLE],
        out_specs=[WHOLE, WHOLE],
        out_shape=[shape, shape],
        compiler_params=params(16),
        cost_estimate=pl.CostEstimate(flops=1 << 21, bytes_accessed=6 << 20, transcendentals=0),
        name="finish",
    )(coef, step, trans, below, above, w)


def swap(chunks):
    return lax.all_to_all(chunks, "comp", split_axis=0, concat_axis=0, tiled=True)


def neighbours(low, top):
    count = lax.axis_size("ctr")
    below = lax.ppermute(top, "ctr", [(i, i + 1) for i in range(count - 1)])
    above = lax.ppermute(low, "ctr", [(i + 1, i) for i in range(count - 1)])
    return below, above


def level_coefs(level_rate, level_code, levels):
    hop = level_code - 2 + (level_code >= 2).astype(jnp.int32)
    target = jnp.arange(level_rate.shape[0], dtype=jnp.int32) + hop
    live = (target >= 0) & (target < level_rate.shape[0])
    out_rate = jnp.where(live, level_rate, F32(0.0))
    total = level_rate.shape[0]
    rows = []
    for offset in OFFSETS:
        source = jnp.pad(jnp.where(hop == offset, level_rate, F32(0.0)), 2)
        rows.append(source[2 - offset : 2 - offset + total])
    table = jnp.stack(rows + [out_rate])
    start = lax.axis_index("ctr") * levels
    return lax.dynamic_slice_in_dim(table, start, levels, axis=1), jnp.max(out_rate)


def local(initial, rates_first, blocks_first, rates_second, blocks_second, level_rate, level_code):
    levels, rows, order = initial.shape
    count = lax.axis_size("comp")
    parts = order // LANES
    chunks = initial.reshape(levels, rows, parts, LANES).transpose(0, 2, 1, 3)
    turned_mass = swap(chunks.reshape(count, rows, LANES)).reshape(order, LANES)

    below, above = neighbours(initial[:2], initial[levels - 2 :])
    sec_high, sec_low, sec_exits = expand(rates_second, blocks_second, True)
    fst_high, fst_low, fst_exits = expand(rates_first, blocks_first, False)
    table, top_rate = level_coefs(level_rate, level_code, levels)
    uniform_rate = jnp.max(fst_exits) + jnp.max(sec_exits) + top_rate
    scale = 1.0 / uniform_rate
    coef = jnp.concatenate([table, jnp.full((1, levels), scale, F32)])
    scale = scale.reshape(1)
    exits = fst_exits.reshape(1, order)
    bv = first(fst_high, fst_low, exits, coef, initial, below, above)

    w_one = turned(sec_high, sec_low, sec_exits, scale, turned_mass)
    back_one = swap(w_one.reshape(count, rows, LANES))
    w_two = turned(sec_high, sec_low, sec_exits, scale, w_one)
    back_two = swap(w_two.reshape(count, rows, LANES))

    s, low, top = gather(bv, back_one)
    s_below, s_above = neighbours(low, top)
    step, trans = twice(fst_high, fst_low, exits, coef, initial, bv, s)
    transient, stepped = finish(coef, step, trans, s_below, s_above, back_two)
    return transient, stepped


def solution(mesh):
    placed = (P("ctr", "comp", None), P(), P(), P(), P(), P(), P())
    return jax.shard_map(
        local,
        mesh=mesh,
        in_specs=placed,
        out_specs=(P("ctr", "comp", None), P("ctr", "comp", None)),
        check_vma=False,
    )
```

profile of v0, /device:TPU:1, one launch (start us, length us, event | category | flops | bytes accessed | tf_op | source)
XLA Modules:
  0.0 122.6 jit_solution(984871276106377939)
XLA Ops:
  3.0 12.2 %all-to-all-start = ((f32[32,32,256]{2,1,0:T(8,128)}), f32[32,32,256]{2,1,0:T(8,128)}, u32[]{:S(2)}, u32[]{:S(2)}) async-start(f32[32,32,256]{2,1,0:T(8,128)} %bitcast.6), calls=%async_computation | async-start | bytes 2097152 | tf_op jit(solution)/shard_map/all_to_all | solution.py:239
  15.1 2.2 %copy-done.8 = f32[1024,1024]{1,0:T(8,128)S(1)} copy-done((f32[1024,1024]{1,0:T(8,128)S(1)}, f32[1024,1024]{1,0:T(8,128)}, u32[]{:S(2)}) %copy-start.8) | copy-done | bytes 4194328
  17.3 3.6 %expand_turned.1 = (bf16[1024,1024]{1,0:T(8,128)(2,1)S(1)}, bf16[1024,1024]{1,0:T(8,128)(2,1)S(1)}, f32[1024,1]{1,0:T(8,128)S(1)}) custom-call(f32[1024,1024]{1,0:T(8,128)S(1)} %copy-done.8, s32[16,16]{1,0:T(8,128)S(1)} %copy-done.15), custom_call_target="tpu_custom_call" | custom-call | flops 67108864 | bytes 8388608 | tf_op jit(solution)/shard_map/expand_turned/pallas_call | solution.py:56
  21.0 1.3 %copy-done.1 = bf16[1024,1024]{1,0:T(8,128)(2,1)} copy-done((bf16[1024,1024]{1,0:T(8,128)(2,1)}, bf16[1024,1024]{1,0:T(8,128)(2,1)S(1)}, u32[]{:S(2)}) %copy-start.1) | copy-done | bytes 2097176
  23.1 2.2 %copy-done.9 = f32[1024,1024]{1,0:T(8,128)S(1)} copy-done((f32[1024,1024]{1,0:T(8,128)S(1)}, f32[1024,1024]{1,0:T(8,128)}, u32[]{:S(2)}) %copy-start.9) | copy-done | bytes 4194328
  25.3 2.1 %expand.1 = (bf16[1024,1024]{1,0:T(8,128)(2,1)S(1)}, bf16[1024,1024]{1,0:T(8,128)(2,1)S(1)}, f32[1024,1]{1,0:T(8,128)S(1)}) custom-call(f32[1024,1024]{1,0:T(8,128)S(1)} %copy-done.9, s32[16,16]{1,0:T(8,128)S(1)} %copy-done.16), custom_call_target="tpu_custom_call" | custom-call | flops 67108864 | bytes 8388608 | tf_op jit(solution)/shard_map/expand/pallas_call | solution.py:56
  33.4 6.3 %all-to-all-done = f32[32,32,256]{2,1,0:T(8,128)} async-done(((f32[32,32,256]{2,1,0:T(8,128)}), f32[32,32,256]{2,1,0:T(8,128)}, u32[]{:S(2)}, u32[]{:S(2)}) %all-to-all-start) | async-done | bytes 1048608 | tf_op jit(solution)/shard_map/all_to_all | solution.py:239
  39.7 1.6 %copy-done.2 = bf16[1024,1024]{1,0:T(8,128)(2,1)S(1)} copy-done((bf16[1024,1024]{1,0:T(8,128)(2,1)S(1)}, bf16[1024,1024]{1,0:T(8,128)(2,1)}, u32[]{:S(2)}) %copy-start.2) | copy-done | bytes 2097176
  41.3 4.0 %second.2.mass_ref = f32[1024,256]{1,0:T(8,128)} custom-call(bf16[1024,1024]{1,0:T(8,128)(2,1)S(1)} %get-tuple-element.17.high_ref, bf16[1024,1024]{1,0:T(8,128)(2,1)S(1)} %copy-done.2, f32[1024,1]{1,0:T(8,128)S(1)} %get-tuple-element.14.exits_ref, f32[1]{0:T(128)} %bitcast.5.scale_ref, f32[1024,256]{1,0:T(8,128)} %bitcast.7.mass_ref), custom_call_target="tpu_custom_call" | custom-call | flops 1610612736 | bytes 6291456 | tf_op jit(solution)/shard_map/second/pallas_call | solution.py:84
  45.3 8.7 %all-to-all-start.1 = ((f32[32,32,256]{2,1,0:T(8,128)}), f32[32,32,256]{2,1,0:T(8,128)}, u32[]{:S(2)}, u32[]{:S(2)}) async-start(f32[32,32,256]{2,1,0:T(8,128)} %bitcast.8), calls=%async_computation.1 | async-start | bytes 2097152 | tf_op jit(solution)/shard_map/all_to_all | solution.py:239
  54.0 1.6 %copy-done.3 = bf16[1024,1024]{1,0:T(8,128)(2,1)S(1)} copy-done((bf16[1024,1024]{1,0:T(8,128)(2,1)S(1)}, bf16[1024,1024]{1,0:T(8,128)(2,1)}, u32[]{:S(2)}) %copy-start.3) | copy-done | bytes 2097176
  55.6 3.0 %second.3 = f32[1024,256]{1,0:T(8,128)S(1)} custom-call(bf16[1024,1024]{1,0:T(8,128)(2,1)S(1)} %get-tuple-element.17.high_ref, bf16[1024,1024]{1,0:T(8,128)(2,1)S(1)} %copy-done.3, f32[1024,1]{1,0:T(8,128)S(1)} %get-tuple-element.14.exits_ref, f32[1]{0:T(128)} %bitcast.5.scale_ref, f32[1024,256]{1,0:T(8,128)} %second.2.mass_ref), custom_call_target="tpu_custom_call" | custom-call | flops 1610612736 | bytes 6291456 | tf_op jit(solution)/shard_map/second/pallas_call | solution.py:84
  59.6 19.1 %all-to-all-done.1.w_ref = f32[32,32,256]{2,1,0:T(8,128)} async-done(((f32[32,32,256]{2,1,0:T(8,128)}), f32[32,32,256]{2,1,0:T(8,128)}, u32[]{:S(2)}, u32[]{:S(2)}) %all-to-all-start.1) | async-done | bytes 1048608 | tf_op jit(solution)/shard_map/all_to_all | solution.py:239
  78.8 8.6 %all-to-all-start.2 = ((f32[32,32,256]{2,1,0:T(8,128)}), f32[32,32,256]{2,1,0:T(8,128)}, u32[]{:S(2)}, u32[]{:S(2)}) async-start(f32[32,32,256]{2,1,0:T(8,128)} %bitcast.15), calls=%async_computation.2 | async-start | bytes 2097152 | tf_op jit(solution)/shard_map/all_to_all | solution.py:239
  88.2 3.4 %collective-permute-start.1 = (f32[2,32,1024]{2,1,0:T(8,128)}, f32[2,32,1024]{2,1,0:T(8,128)S(1)}, u32[]{:S(2)}, u32[]{:S(2)}) collective-permute-start(f32[2,32,1024]{2,1,0:T(8,128)} %get-tuple-element.32), channel_id=1, source_target_pairs={{32,0},{64,32},{96,64},{128,96},{160,128},{192,160},{224,192},{33,... | collective-permute-start | bytes 786440 | tf_op jit(solution)/shard_map/ppermute | solution.py:245
  91.6 3.0 %collective-permute-start = (f32[2,32,1024]{2,1,0:T(8,128)}, f32[2,32,1024]{2,1,0:T(8,128)}, u32[]{:S(2)}, u32[]{:S(2)}) collective-permute-start(f32[2,32,1024]{2,1,0:T(8,128)} %get-tuple-element.33), channel_id=1, source_target_pairs={{0,32},{32,64},{64,96},{96,128},{128,160},{160,192},{192,224},{1,3... | collective-permute-start | bytes 786440 | tf_op jit(solution)/shard_map/ppermute | solution.py:244
  94.8 2.5 %collective-permute-done.1.above_ref = f32[2,32,1024]{2,1,0:T(8,128)S(1)} collective-permute-done((f32[2,32,1024]{2,1,0:T(8,128)}, f32[2,32,1024]{2,1,0:T(8,128)S(1)}, u32[]{:S(2)}, u32[]{:S(2)}) %collective-permute-start.1) | collective-permute-done | bytes 262176 | tf_op jit(solution)/shard_map/ppermute | solution.py:245
  98.2 1.6 %copy-done.7 = bf16[1024,1024]{1,0:T(8,128)(2,1)S(1)} copy-done((bf16[1024,1024]{1,0:T(8,128)(2,1)S(1)}, bf16[1024,1024]{1,0:T(8,128)(2,1)}, u32[]{:S(2)}) %copy-start.7) | copy-done | bytes 2097176
  99.8 3.0 %first.1.bv_ref = f32[8,32,1024]{2,1,0:T(8,128)S(1)} custom-call(bf16[1024,1024]{1,0:T(8,128)(2,1)S(1)} %copy-done.5, bf16[1024,1024]{1,0:T(8,128)(2,1)S(1)} %copy-done.7, f32[1,1024]{1,0:T(1,128)S(1)} %bitcast.16, f32[6,8]{1,0:T(8,128)S(1)} %concatenate.6.coef_ref, f32[8,32,1024]{2,1,0:T(8,128)S(1)} %copy-done, ...), custom_call_target="tpu_custom_call" | custom-call | flops 1610612736 | bytes 7340032 | tf_op jit(solution)/shard_map/first/pallas_call | solution.py:132
  102.8 2.2 %once.1 = (f32[8,32,1024]{2,1,0:T(8,128)S(1)}, f32[2,32,1024]{2,1,0:T(8,128)}, f32[2,32,1024]{2,1,0:T(8,128)}) custom-call(f32[8,32,1024]{2,1,0:T(8,128)S(1)} %first.1.bv_ref, f32[32,32,256]{2,1,0:T(8,128)} %all-to-all-done.1.w_ref), custom_call_target="tpu_custom_call" | custom-call | flops 1048576 | bytes 4194304 | tf_op jit(solution)/shard_map/once/pallas_call | solution.py:160
  104.9 4.4 %collective-permute-start.2 = (f32[2,32,1024]{2,1,0:T(8,128)}, f32[2,32,1024]{2,1,0:T(8,128)S(1)}, u32[]{:S(2)}, u32[]{:S(2)}) collective-permute-start(f32[2,32,1024]{2,1,0:T(8,128)} %get-tuple-element.22), channel_id=1, source_target_pairs={{0,32},{32,64},{64,96},{96,128},{128,160},{160,192},{192,224},{1,3... | collective-permute-start | bytes 786440 | tf_op jit(solution)/shard_map/ppermute | solution.py:244
  109.3 1.9 %collective-permute-start.3 = (f32[2,32,1024]{2,1,0:T(8,128)}, f32[2,32,1024]{2,1,0:T(8,128)}, u32[]{:S(2)}, u32[]{:S(2)}) collective-permute-start(f32[2,32,1024]{2,1,0:T(8,128)} %get-tuple-element.23), channel_id=1, source_target_pairs={{32,0},{64,32},{96,64},{128,96},{160,128},{192,160},{224,192},{33,... | collective-permute-start | bytes 786440 | tf_op jit(solution)/shard_map/ppermute | solution.py:245
  111.3 2.8 %twice.1 = (f32[8,32,1024]{2,1,0:T(8,128)S(1)}, f32[8,32,1024]{2,1,0:T(8,128)S(1)}) custom-call(bf16[1024,1024]{1,0:T(8,128)(2,1)S(1)} %copy-done.5, bf16[1024,1024]{1,0:T(8,128)(2,1)S(1)} %copy-done.7, f32[1,1024]{1,0:T(1,128)S(1)} %bitcast.17, f32[6,8]{1,0:T(8,128)S(1)} %concatenate.6.coef_ref, f32[8,32,1024]{2,1,0:T(8,128)S(1)} %copy-done, ...), custom_call_target="tpu_custom_call" | custom-call | flops 1610612736 | bytes 9437184 | tf_op jit(solution)/shard_map/twice/pallas_call | solution.py:193
  119.8 2.9 %finish.1 = (f32[8,32,1024]{2,1,0:T(8,128)}, f32[8,32,1024]{2,1,0:T(8,128)}) custom-call(f32[6,8]{1,0:T(8,128)S(1)} %concatenate.6.coef_ref, f32[8,32,1024]{2,1,0:T(8,128)S(1)} %copy-done.12, f32[8,32,1024]{2,1,0:T(8,128)S(1)} %copy-done.14, f32[2,32,1024]{2,1,0:T(8,128)S(1)} %collective-permute-done.2.below_ref, ...), custom_call_target="tpu_custom_call" | custom-call | flops 2097152 | bytes 6291456 | tf_op jit(solution)/shard_map/finish/pallas_call | solution.py:227
  (47 shorter events, 15.8 us)
Async XLA Ops:
  1.9 13.2 %copy-start.15 = (s32[16,16]{1,0:T(8,128)S(1)}, s32[16,16]{1,0:T(8,128)}, u32[]{:S(2)}) copy-start(s32[16,16]{1,0:T(8,128)} %blocks_ref.3) | copy-start | bytes 3076
  3.0 36.8 %all-to-all-start = ((f32[32,32,256]{2,1,0:T(8,128)}), f32[32,32,256]{2,1,0:T(8,128)}, u32[]{:S(2)}, u32[]{:S(2)}) async-start(f32[32,32,256]{2,1,0:T(8,128)} %bitcast.6), calls=%async_computation | async-start | bytes 2097152 | tf_op jit(solution)/shard_map/all_to_all | solution.py:239
  15.1 2.2 %copy-start.8 = (f32[1024,1024]{1,0:T(8,128)S(1)}, f32[1024,1024]{1,0:T(8,128)}, u32[]{:S(2)}) copy-start(f32[1024,1024]{1,0:T(8,128)} %rates_ref.3) | copy-start | bytes 12582916
  17.3 5.8 %copy-start.16 = (s32[16,16]{1,0:T(8,128)S(1)}, s32[16,16]{1,0:T(8,128)}, u32[]{:S(2)}) copy-start(s32[16,16]{1,0:T(8,128)} %blocks_ref.2) | copy-start | bytes 3076
  21.0 1.4 %copy-start.1 = (bf16[1024,1024]{1,0:T(8,128)(2,1)}, bf16[1024,1024]{1,0:T(8,128)(2,1)S(1)}, u32[]{:S(2)}) copy-start(bf16[1024,1024]{1,0:T(8,128)(2,1)S(1)} %get-tuple-element.18.low_ref) | copy-start | bytes 6291460
  23.1 2.2 %copy-start.9 = (f32[1024,1024]{1,0:T(8,128)S(1)}, f32[1024,1024]{1,0:T(8,128)}, u32[]{:S(2)}) copy-start(f32[1024,1024]{1,0:T(8,128)} %rates_ref.2) | copy-start | bytes 12582916
  25.3 6.8 %copy-start.17 = (f32[64]{0:T(128)S(1)}, f32[64]{0:T(128)}, u32[]{:S(2)}) copy-start(f32[64]{0:T(128)} %param.12) | copy-start | bytes 772
  25.3 6.8 %copy-start.18 = (s32[64]{0:T(128)S(1)}, s32[64]{0:T(128)}, u32[]{:S(2)}) copy-start(s32[64]{0:T(128)} %param.13) | copy-start | bytes 772
  27.4 1.3 %copy-start.4 = (bf16[1024,1024]{1,0:T(8,128)(2,1)}, bf16[1024,1024]{1,0:T(8,128)(2,1)S(1)}, u32[]{:S(2)}) copy-start(bf16[1024,1024]{1,0:T(8,128)(2,1)S(1)} %get-tuple-element.15.high_ref) | copy-start | bytes 6291460
  28.8 1.3 %copy-start.6 = (bf16[1024,1024]{1,0:T(8,128)(2,1)}, bf16[1024,1024]{1,0:T(8,128)(2,1)S(1)}, u32[]{:S(2)}) copy-start(bf16[1024,1024]{1,0:T(8,128)(2,1)S(1)} %get-tuple-element.16.low_ref) | copy-start | bytes 6291460
  39.7 1.6 %copy-start.2 = (bf16[1024,1024]{1,0:T(8,128)(2,1)S(1)}, bf16[1024,1024]{1,0:T(8,128)(2,1)}, u32[]{:S(2)}) copy-start(bf16[1024,1024]{1,0:T(8,128)(2,1)} %copy-done.1) | copy-start | bytes 6291460
  45.3 33.5 %all-to-all-start.1 = ((f32[32,32,256]{2,1,0:T(8,128)}), f32[32,32,256]{2,1,0:T(8,128)}, u32[]{:S(2)}, u32[]{:S(2)}) async-start(f32[32,32,256]{2,1,0:T(8,128)} %bitcast.8), calls=%async_computation.1 | async-start | bytes 2097152 | tf_op jit(solution)/shard_map/all_to_all | solution.py:239
  54.0 1.6 %copy-start.3 = (bf16[1024,1024]{1,0:T(8,128)(2,1)S(1)}, bf16[1024,1024]{1,0:T(8,128)(2,1)}, u32[]{:S(2)}) copy-start(bf16[1024,1024]{1,0:T(8,128)(2,1)} %copy-done.1) | copy-start | bytes 6291460
  58.7 1.0 copy-start.10
  59.6 27.7 %copy-start = (f32[8,32,1024]{2,1,0:T(8,128)S(1)}, f32[8,32,1024]{2,1,0:T(8,128)}, u32[]{:S(2)}) copy-start(f32[8,32,1024]{2,1,0:T(8,128)} %v_ref.3) | copy-start | bytes 3145732
  59.6 38.6 %copy-start.5 = (bf16[1024,1024]{1,0:T(8,128)(2,1)S(1)}, bf16[1024,1024]{1,0:T(8,128)(2,1)}, u32[]{:S(2)}) copy-start(bf16[1024,1024]{1,0:T(8,128)(2,1)} %copy-done.4) | copy-start | bytes 6291460
  78.8 37.2 %all-to-all-start.2 = ((f32[32,32,256]{2,1,0:T(8,128)}), f32[32,32,256]{2,1,0:T(8,128)}, u32[]{:S(2)}, u32[]{:S(2)}) async-start(f32[32,32,256]{2,1,0:T(8,128)} %bitcast.15), calls=%async_computation.2 | async-start | bytes 2097152 | tf_op jit(solution)/shard_map/all_to_all | solution.py:239
  88.2 9.1 %collective-permute-start.1 = (f32[2,32,1024]{2,1,0:T(8,128)}, f32[2,32,1024]{2,1,0:T(8,128)S(1)}, u32[]{:S(2)}, u32[]{:S(2)}) collective-permute-start(f32[2,32,1024]{2,1,0:T(8,128)} %get-tuple-element.32), channel_id=1, source_target_pairs={{32,0},{64,32},{96,64},{128,96},{160,128},{192,160},{224,192},{33,... | collective-permute-start | bytes 786440 | tf_op jit(solution)/shard_map/ppermute | solution.py:245
  91.6 6.6 %collective-permute-start = (f32[2,32,1024]{2,1,0:T(8,128)}, f32[2,32,1024]{2,1,0:T(8,128)}, u32[]{:S(2)}, u32[]{:S(2)}) collective-permute-start(f32[2,32,1024]{2,1,0:T(8,128)} %get-tuple-element.33), channel_id=1, source_target_pairs={{0,32},{32,64},{64,96},{96,128},{128,160},{160,192},{192,224},{1,3... | collective-permute-start | bytes 786440 | tf_op jit(solution)/shard_map/ppermute | solution.py:244
  98.2 1.6 %copy-start.7 = (bf16[1024,1024]{1,0:T(8,128)(2,1)S(1)}, bf16[1024,1024]{1,0:T(8,128)(2,1)}, u32[]{:S(2)}) copy-start(bf16[1024,1024]{1,0:T(8,128)(2,1)} %copy-done.6) | copy-start | bytes 6291460
  104.9 11.1 %collective-permute-start.2 = (f32[2,32,1024]{2,1,0:T(8,128)}, f32[2,32,1024]{2,1,0:T(8,128)S(1)}, u32[]{:S(2)}, u32[]{:S(2)}) collective-permute-start(f32[2,32,1024]{2,1,0:T(8,128)} %get-tuple-element.22), channel_id=1, source_target_pairs={{0,32},{32,64},{64,96},{96,128},{128,160},{160,192},{192,224},{1,3... | collective-permute-start | bytes 786440 | tf_op jit(solution)/shard_map/ppermute | solution.py:244
  109.3 8.0 %collective-permute-start.3 = (f32[2,32,1024]{2,1,0:T(8,128)}, f32[2,32,1024]{2,1,0:T(8,128)}, u32[]{:S(2)}, u32[]{:S(2)}) collective-permute-start(f32[2,32,1024]{2,1,0:T(8,128)} %get-tuple-element.23), channel_id=1, source_target_pairs={{32,0},{64,32},{96,64},{128,96},{160,128},{192,160},{224,192},{33,... | collective-permute-start | bytes 786440 | tf_op jit(solution)/shard_map/ppermute | solution.py:245
  117.3 1.2 copy-start.12
  118.6 1.2 copy-start.14
  (2 other events, 1.9 us)
where the time goes:
time: 124 us; the launch traced here: 123 us
  starting transfers between devices  42.1 us (34%)
  waiting for transfers between devices  30.1 us (24%)
  Pallas kernels  23.5 us (19%)
  local copies, waits for them, and re-layouts  20.8 us (17%)
  other arithmetic  3.18 us (3%)
  between operations  2.85 us (2%)
    all_to_all x3, starting transfers between devices, swap(): lax.all_to_all(chunks, 'comp', split_axis=0, concat_axis=0, tiled=True)  29.4 us
    all_to_all x3, waiting for transfers between devices, swap(): lax.all_to_all(chunks, 'comp', split_axis=0, concat_axis=0, tiled=True)  25.4 us
    unnamed x38, local copies, waits for them, and re-layouts  18.5 us
    ppermute x2, starting transfers between devices, neighbours(): below = lax.ppermute(top, 'ctr', [(i, i + 1) for i in range(count - 1)])  7.4 us
    pallas_call x2, Pallas kernels, turned(): pl.pallas_call(turned_kernel, in_specs=[WHOLE, WHOLE, WHOLE, SCALARS, WHO...  7.02 us
    pallas_call x2, Pallas kernels, expand(): pl.pallas_call(functools.partial(expand_kernel, turn), grid=(order // tal...  5.73 us
    ppermute x2, starting transfers between devices, neighbours(): above = lax.ppermute(low, 'ctr', [(i + 1, i) for i in range(count - 1)])  5.28 us
    ppermute x2, waiting for transfers between devices, neighbours(): above = lax.ppermute(low, 'ctr', [(i + 1, i) for i in range(count - 1)])  3.79 us
  transfers between devices with their start and end apart: 7, of which 5 were waited for; matrix products, arithmetic and copies ran while one was open for 3% of the time, Pallas kernels for 14%

commit v1 on v0

v1 whole, which is shorter than its diff:
```python
import functools

import jax
import jax.numpy as jnp
from jax import lax
from jax.experimental import pallas as pl
from jax.experimental.pallas import tpu as pltpu
from jax.sharding import PartitionSpec as P

F32 = jnp.float32
BF16 = jnp.bfloat16
LANES = 256
SIDE = 4
OFFSETS = (-2, -1, 1, 2)
HBM = pl.BlockSpec(memory_space=pltpu.HBM)
WHOLE = pl.BlockSpec(memory_space=pltpu.VMEM)
SCALARS = pl.BlockSpec(memory_space=pltpu.SMEM)


def params(mib):
    return pltpu.CompilerParams(vmem_limit_bytes=mib << 20)


def halves(x):
    high = x.astype(BF16)
    return high, (x - high.astype(F32)).astype(BF16)


def mm(a, b):
    return jnp.dot(a, b, preferred_element_type=F32)


def mask_rows(blocks_ref, row, tall, order):
    nblk = blocks_ref.shape[0]
    left = (row == lax.broadcasted_iota(jnp.int32, (tall, nblk), 1)).astype(BF16)
    col = lax.broadcasted_iota(jnp.int32, (nblk, order), 1) // (order // nblk)
    right = (col == lax.broadcasted_iota(jnp.int32, (nblk, order), 0)).astype(BF16)
    wide = mm(blocks_ref[...].astype(F32).astype(BF16), right).astype(BF16)
    return mm(left, wide)


def coefficients(rate_ref, code_ref, rate_row_ref, code_row_ref, start_ref, tops, coef_ref):
    total = rate_row_ref.shape[1]
    levels = coef_ref.shape[1]
    start = start_ref[0]
    code = code_row_ref[...]
    target = lax.broadcasted_iota(jnp.int32, code.shape, 1) + code - 2 + (code >= 2).astype(jnp.int32)
    live = (target >= 0) & (target < total)
    top = jnp.max(jnp.where(live, rate_row_ref[...], F32(0.0)))
    scale = 1.0 / (tops[0] + tops[1] + top)

    def hop(n):
        return code_ref[n] - 2 + jnp.where(code_ref[n] >= 2, 1, 0)

    for m in range(levels):
        here = start + m
        for k, offset in enumerate(OFFSETS):
            n = here - offset
            at = jnp.clip(n, 0, total - 1)
            good = (n >= 0) & (n < total) & (hop(at) == offset)
            coef_ref[k, m] = jnp.where(good, rate_ref[at], F32(0.0))
        to = here + hop(here)
        coef_ref[4, m] = jnp.where((to >= 0) & (to < total), rate_ref[here], F32(0.0))
        coef_ref[5, m] = scale


def prepare_kernel(
    rate_ref, code_ref, start_ref, rate_row_ref, code_row_ref, fst_ref, fst_blocks_ref, sec_ref, sec_blocks_ref,
    fst_high, fst_low, fst_exits, sec_both, sec_exits, coef_ref, tops,
):
    step = pl.program_id(0)
    tall, order = fst_ref.shape
    nblk = fst_blocks_ref.shape[0]
    width = order // nblk
    at = lax.broadcasted_iota(jnp.int32, (tall, nblk), 0)
    full = fst_ref[...] * mask_rows(fst_blocks_ref, at // width + step * (tall // width), tall, order)
    sums = jnp.sum(full, axis=1, keepdims=True)
    fst_exits[...] = jnp.broadcast_to(sums, (tall, 128)).T[:8]
    fst_high[...], fst_low[...] = halves(full)
    top_first = jnp.max(sums)

    side, along, rows, _ = sec_ref.shape
    deep = order // (side * rows)
    row = ((at // rows % side) * deep + at // (rows * side) + step * along) * rows // width
    pieces = [sec_ref[y, z] for z in range(along) for y in range(side)]
    full = jnp.concatenate(pieces, axis=0) * mask_rows(sec_blocks_ref, row, tall, order)
    sums = jnp.sum(full, axis=1, keepdims=True)
    sec_exits[:, pl.ds(pl.multiple_of(step * tall, tall), tall)] = jnp.broadcast_to(sums, (tall, 128)).T[:8]
    turn = full.T
    for z in range(deep):
        for y in range(side):
            block = turn[(y * deep + z) * rows : (y * deep + z + 1) * rows]
            to = pl.ds((z * side + y) * rows, rows)
            sec_both[0, to, :], sec_both[1, to, :] = halves(block)
    top_second = jnp.max(sums)

    @pl.when(step == 0)
    def _():
        tops[0] = top_first
        tops[1] = top_second

    @pl.when(step > 0)
    def _():
        tops[0] = jnp.maximum(tops[0], top_first)
        tops[1] = jnp.maximum(tops[1], top_second)

    @pl.when(step == pl.num_programs(0) - 1)
    def _():
        coefficients(rate_ref, code_ref, rate_row_ref, code_row_ref, start_ref, tops, coef_ref)
        sec_exits[4:8, :] = jnp.full((4, sec_exits.shape[1]), coef_ref[5, 0], F32)


def prepare(level_rate, level_code, start, rates_first, blocks_first, rates_second, blocks_second, levels, count, tall=256):
    order = rates_first.shape[0]
    total = level_rate.shape[0]
    rows = pl.BlockSpec((tall, order), lambda i: (i, 0))
    both = pl.BlockSpec((2, order, tall), lambda i: (0, 0, i))
    small = pl.BlockSpec(blocks_first.shape, lambda i: (0, 0))
    line = pl.BlockSpec((1, total), lambda i: (0, 0))
    half = jax.ShapeDtypeStruct((order, order), BF16)
    deep = count // SIDE
    along = tall // (SIDE * (order // count))
    pieces = pl.BlockSpec((SIDE, along, order // count, order), lambda i: (0, i, 0, 0))
    return pl.pallas_call(
        prepare_kernel,
        grid=(order // tall,),
        in_specs=[SCALARS, SCALARS, SCALARS, line, line, rows, small, pieces, small],
        out_specs=[
            rows, rows, pl.BlockSpec((8, tall), lambda i: (0, i)),
            both, pl.BlockSpec((8, order), lambda i: (0, 0)), SCALARS,
        ],
        out_shape=[
            half, half, jax.ShapeDtypeStruct((8, order), F32),
            jax.ShapeDtypeStruct((2, order, order), BF16),
            jax.ShapeDtypeStruct((8, order), F32), jax.ShapeDtypeStruct((6, levels), F32),
        ],
        scratch_shapes=[pltpu.SMEM((2,), F32)],
        compiler_params=params(60),
        cost_estimate=pl.CostEstimate(flops=1 << 27, bytes_accessed=16 << 20, transcendentals=0),
        name="prepare",
    )(
        level_rate, level_code, start, level_rate.reshape(1, total), level_code.reshape(1, total),
        rates_first, blocks_first, rates_second.reshape(SIDE, deep, order // count, order), blocks_second,
    )


def turned_kernel(both_ref, exits_ref, mass_ref, out_ref, up, down):
    @pl.when(pl.program_id(0) == 0)
    def _():
        up[...], down[...] = halves(mass_ref[...])

    tall = out_ref.shape[0]
    rows = pl.ds(pl.multiple_of(pl.program_id(0) * tall, tall), tall)
    left = both_ref[0]
    total = mm(left, up[...]) + mm(left, down[...]) + mm(both_ref[1], up[...])
    turn = exits_ref[...].T
    out_ref[...] = (total - mass_ref[rows, :] * turn[:, 0:1]) * turn[:, 4:5]


def turned(both, exits, mass, tall=512):
    order, width = mass.shape
    return pl.pallas_call(
        turned_kernel,
        grid=(order // tall,),
        in_specs=[
            pl.BlockSpec((2, tall, order), lambda i: (0, i, 0)),
            pl.BlockSpec((8, tall), lambda i: (0, i)),
            pl.BlockSpec((order, width), lambda i: (0, 0)),
        ],
        out_specs=pl.BlockSpec((tall, width), lambda i: (i, 0)),
        out_shape=jax.ShapeDtypeStruct(mass.shape, F32),
        scratch_shapes=[pltpu.VMEM((order, width), BF16), pltpu.VMEM((order, width), BF16)],
        compiler_params=params(60),
        cost_estimate=pl.CostEstimate(flops=3 << 29, bytes_accessed=6 << 20, transcendentals=0),
        name="second",
    )(both, exits, mass)


def product(x, high_ref, low_ref, cols):
    high, low = x
    return mm(high, high_ref[:, cols]) + mm(low, high_ref[:, cols]) + mm(high, low_ref[:, cols])


def hops(coef_ref, m, get, levels):
    total = None
    for k, offset in enumerate(OFFSETS):
        source = get(m - offset)
        if source is not None:
            part = coef_ref[k, m] * source
            total = part if total is None else total + part
    return total


def first_kernel(high_ref, low_ref, exits_ref, coef_ref, v_ref, below_ref, above_ref, out_ref):
    levels, rows, order = v_ref.shape
    x = halves(v_ref[...].reshape(levels * rows, order))
    scale = coef_ref[5, 0]
    for at in range(0, order, 256):
        cols = pl.ds(at, 256)
        prod = product(x, high_ref, low_ref, cols).reshape(levels, rows, 256)

        def get(n, cols=cols):
            if n < 0:
                return below_ref[n + 2, :, cols]
            if n >= levels:
                return above_ref[n - levels, :, cols]
            return v_ref[n, :, cols]

        for m in range(levels):
            here = v_ref[m, :, cols]
            change = prod[m] - here * (exits_ref[0:1, cols] + coef_ref[4, m])
            out_ref[m, :, cols] = here + scale * (change + hops(coef_ref, m, get, levels))


def first(high, low, exits, coef, v, below, above):
    return pl.pallas_call(
        first_kernel,
        in_specs=[WHOLE, WHOLE, WHOLE, SCALARS, WHOLE, WHOLE, WHOLE],
        out_specs=WHOLE,
        out_shape=jax.ShapeDtypeStruct(v.shape, F32),
        compiler_params=params(20),
        cost_estimate=pl.CostEstimate(flops=3 << 29, bytes_accessed=7 << 20, transcendentals=0),
        name="first",
    )(high, low, exits, coef, v, below, above)


def gather_kernel(bv_ref, w_ref, sum_ref, low_ref, top_ref):
    levels, _, order = bv_ref.shape
    parts = order // LANES
    for m in range(levels):
        for p in range(parts):
            cols = pl.ds(p * LANES, LANES)
            s = bv_ref[m, :, cols] + 2.0 * w_ref[m * parts + p]
            sum_ref[m, :, cols] = s
            if m < 2:
                low_ref[m, :, cols] = s
            if m >= levels - 2:
                top_ref[m - levels + 2, :, cols] = s


def gather(bv, w):
    levels, rows, order = bv.shape
    edge = jax.ShapeDtypeStruct((2, rows, order), F32)
    return pl.pallas_call(
        gather_kernel,
        in_specs=[WHOLE, WHOLE],
        out_specs=[WHOLE, WHOLE, WHOLE],
        out_shape=[jax.ShapeDtypeStruct(bv.shape, F32), edge, edge],
        compiler_params=params(12),
        cost_estimate=pl.CostEstimate(flops=1 << 20, bytes_accessed=4 << 20, transcendentals=0),
        name="once",
    )(bv, w)


def twice_kernel(high_ref, low_ref, exits_ref, coef_ref, v_ref, bv_ref, s_ref, below_ref, above_ref, step_ref, trans_ref):
    levels, rows, order = v_ref.shape
    x = halves(s_ref[...].reshape(levels * rows, order))
    scale = coef_ref[5, 0]
    for at in range(0, order, 256):
        cols = pl.ds(at, 256)
        prod = product(x, high_ref, low_ref, cols).reshape(levels, rows, 256)

        def get(n, cols=cols):
            if n < 0:
                return below_ref[n + 2, :, cols]
            if n >= levels:
                return above_ref[n - levels, :, cols]
            return s_ref[n, :, cols]

        for m in range(levels):
            here = s_ref[m, :, cols]
            change = prod[m] - here * (exits_ref[0:1, cols] + coef_ref[4, m])
            stepped = here + scale * (change + hops(coef_ref, m, get, levels))
            once = 0.5 * (here + bv_ref[m, :, cols])
            step_ref[m, :, cols] = stepped
            trans_ref[m, :, cols] = (v_ref[m, :, cols] + once) * 0.4 + 0.2 * stepped


def twice(high, low, exits, coef, v, bv, s, below, above):
    shape = jax.ShapeDtypeStruct(v.shape, F32)
    return pl.pallas_call(
        twice_kernel,
        in_specs=[WHOLE, WHOLE, WHOLE, SCALARS, WHOLE, WHOLE, WHOLE, WHOLE, WHOLE],
        out_specs=[WHOLE, WHOLE],
        out_shape=[shape, shape],
        compiler_params=params(24),
        cost_estimate=pl.CostEstimate(flops=3 << 29, bytes_accessed=9 << 20, transcendentals=0),
        name="twice",
    )(high, low, exits, coef, v, bv, s, below, above)


def finish_kernel(step_ref, trans_ref, w_ref, out_t_ref, out_s_ref, step, trans, sems):
    levels, _, order = step_ref.shape
    parts = order // LANES
    pairs = ((step_ref, step, out_s_ref), (trans_ref, trans, out_t_ref))
    loads = [[pltpu.make_async_copy(src.at[m], buf.at[m], sems.at[m, k]) for k, (src, buf, _) in enumerate(pairs)] for m in range(levels)]
    stores = [[pltpu.make_async_copy(buf.at[m], dst.at[m], sems.at[m, 2 + k]) for k, (_, buf, dst) in enumerate(pairs)] for m in range(levels)]
    for group in loads:
        for load in group:
            load.start()
    for m in range(levels):
        for load in loads[m]:
            load.wait()
        for p in range(parts):
            cols = pl.ds(p * LANES, LANES)
            more = w_ref[m * parts + p]
            step[m, :, cols] = step[m, :, cols] + more
            trans[m, :, cols] = trans[m, :, cols] + 0.2 * more
        for store in stores[m]:
            store.start()
    for group in stores:
        for store in group:
            store.wait()


def finish(step, trans, w):
    shape = jax.ShapeDtypeStruct(step.shape, F32)
    return pl.pallas_call(
        finish_kernel,
        in_specs=[HBM, HBM, WHOLE],
        out_specs=[HBM, HBM],
        out_shape=[shape, shape],
        scratch_shapes=[
            pltpu.VMEM(step.shape, F32),
            pltpu.VMEM(step.shape, F32),
            pltpu.SemaphoreType.DMA((step.shape[0], 4)),
        ],
        compiler_params=params(60),
        cost_estimate=pl.CostEstimate(flops=1 << 20, bytes_accessed=5 << 20, transcendentals=0),
        name="finish",
    )(step, trans, w)


def swap(chunks):
    count = lax.axis_size("comp")
    deep = count // SIDE
    order = [(p % SIDE) * deep + p // SIDE for p in range(count)]
    return lax.all_to_all(chunks, "comp", split_axis=0, concat_axis=0, axis_index_groups=[order], tiled=True)


def neighbours(low, top):
    count = lax.axis_size("ctr")
    below = lax.ppermute(top, "ctr", [(i, i + 1) for i in range(count - 1)])
    above = lax.ppermute(low, "ctr", [(i + 1, i) for i in range(count - 1)])
    return below, above


def local(initial, rates_first, blocks_first, rates_second, blocks_second, level_rate, level_code):
    levels, rows, order = initial.shape
    count = lax.axis_size("comp")
    turned_mass = swap(initial.reshape(levels, rows, order // LANES, LANES).transpose(0, 2, 1, 3).reshape(count, rows, LANES)).reshape(order, LANES)

    below, above = neighbours(initial[:2], initial[levels - 2 :])
    start = (lax.axis_index("ctr") * levels).astype(jnp.int32).reshape(1)
    fst_high, fst_low, exits, sec_both, sec_exits, coef = prepare(
        level_rate, level_code, start, rates_first, blocks_first, rates_second, blocks_second, levels, count
    )
    bv = first(fst_high, fst_low, exits, coef, initial, below, above)

    w_one = turned(sec_both, sec_exits, turned_mass)
    back_one = swap(w_one.reshape(count, rows, LANES))
    w_two = turned(sec_both, sec_exits, w_one)
    w_two, bv = lax.optimization_barrier((w_two, bv))
    back_two = swap(w_two.reshape(count, rows, LANES))

    s, low, top = gather(bv, back_one)
    s_below, s_above = neighbours(low, top)
    step, trans = twice(fst_high, fst_low, exits, coef, initial, bv, s, s_below, s_above)
    transient, stepped = finish(step, trans, back_two)
    return transient, stepped


def solution(mesh):
    placed = (P("ctr", "comp", None), P(), P(), P(), P(), P(), P())
    return jax.shard_map(
        local,
        mesh=mesh,
        in_specs=placed,
        out_specs=(P("ctr", "comp", None), P("ctr", "comp", None)),
        check_vma=False,
    )
```

time: 124 us -> 119 us (0.960)
  the two profiles are of different devices: /device:TPU:1 before, /device:TPU:8 now
where the time goes in v1:
time: 119 us; the launch traced here: 118 us
  waiting for transfers between devices  49 us (41%)
  Pallas kernels  28.8 us (24%)
  starting transfers between devices  28.1 us (24%)
  local copies, waits for them, and re-layouts  10.6 us (9%)
    all_to_all x3, waiting for transfers between devices, swap(): lax.all_to_all(chunks, 'comp', split_axis=0, concat_axis=0, axis_index_gr...  41.3 us
    all_to_all x3, starting transfers between devices, swap(): lax.all_to_all(chunks, 'comp', split_axis=0, concat_axis=0, axis_index_gr...  22.9 us
    pallas_call x2, Pallas kernels, turned(): pl.pallas_call(turned_kernel, grid=(order // tall,), in_specs=[pl.BlockSp...  9.69 us
    pallas_call x1, Pallas kernels, prepare(): pl.pallas_call(prepare_kernel, grid=(order // tall,), in_specs=[SCALARS,...  9.63 us
    unnamed x20, local copies, waits for them, and re-layouts  9.3 us
    ppermute x2, waiting for transfers between devices, neighbours(): above = lax.ppermute(low, 'ctr', [(i + 1, i) for i in range(count - 1)])  7.66 us
    pallas_call x1, Pallas kernels, finish(): pl.pallas_call(finish_kernel, in_specs=[HBM, HBM, WHOLE], out_specs=[HBM,...  3.85 us
    pallas_call x1, Pallas kernels, twice(): pl.pallas_call(twice_kernel, in_specs=[WHOLE, WHOLE, WHOLE, SCALARS, WHOL...  2.89 us
  transfers between devices with their start and end apart: 7, of which 5 were waited for; matrix products, arithmetic and copies ran while one was open for 0% of the time, Pallas kernels for 17%

profile of v1, /device:TPU:8, one launch (start us, length us, event | category | flops | bytes accessed | tf_op | source)
XLA Modules:
  0.0 118.3 jit_solution(5897002019615030710)
XLA Ops:
  0.6 1.3 %fusion.1 = (f32[8,32,256]{2,1,0:T(8,128)S(1)}, f32[8,32,256]{2,1,0:T(8,128)S(1)}, f32[8,32,256]{2,1,0:T(8,128)S(1)}, f32[8,32,256]{2,1,0:T(8,128)S(1)}) fusion(f32[8,32,1024]{2,1,0:T(8,128)} %v_ref.3), kind=kLoop, calls=%fused_computation.2 | loop fusion | bytes 2097152 | tf_op jit(solution)/shard_map/slice
  1.9 1.0 pad_maximum_fusion
  2.9 11.7 %all-to-all-start = ((f32[32,32,256]{2,1,0:T(8,128)}), f32[32,32,256]{2,1,0:T(8,128)S(1)}, u32[]{:S(2)}, u32[]{:S(2)}) async-start(f32[32,32,256]{2,1,0:T(8,128)} %bitcast.4), calls=%async_computation | async-start | bytes 2097152 | tf_op jit(solution)/shard_map/all_to_all | solution.py:338
  14.7 9.6 %prepare.1 = (bf16[1024,1024]{1,0:T(8,128)(2,1)}, bf16[1024,1024]{1,0:T(8,128)(2,1)}, f32[8,1024]{1,0:T(8,128)}, bf16[2,1024,1024]{2,1,0:T(8,128)(2,1)}, f32[8,1024]{1,0:T(8,128)}, /*index=5*/f32[6,8]{1,0:T(8,128)}) custom-call(f32[64]{0:T(128)} %rate_ref.1, s32[64]{0:T(128)} %code_ref.1, s32[1]{0:T(128)} %bitcast.start_ref, f32[1,64]{1,0:T(1,128)} %bitcast.12, ...), custom_call_target="tpu_custom_call" | custom-call | flops 134217728 | bytes 16777216 | tf_op jit(solution)/shard_map/prepare/pallas_call | solution.py:124
  24.3 18.4 %all-to-all-done = f32[32,32,256]{2,1,0:T(8,128)S(1)} async-done(((f32[32,32,256]{2,1,0:T(8,128)}), f32[32,32,256]{2,1,0:T(8,128)S(1)}, u32[]{:S(2)}, u32[]{:S(2)}) %all-to-all-start) | async-done | bytes 1048608 | tf_op jit(solution)/shard_map/all_to_all | solution.py:338
  43.7 4.9 %second.2.mass_ref = f32[1024,256]{1,0:T(8,128)} custom-call(bf16[2,1024,1024]{2,1,0:T(8,128)(2,1)} %get-tuple-element.19.both_ref, f32[8,1024]{1,0:T(8,128)} %get-tuple-element.20.exits_ref, f32[1024,256]{1,0:T(8,128)} %bitcast.11), custom_call_target="tpu_custom_call" | custom-call | flops 1610612736 | bytes 6291456 | tf_op jit(solution)/shard_map/second/pallas_call | solution.py:162
  48.6 5.6 %all-to-all-start.1 = ((f32[32,32,256]{2,1,0:T(8,128)}), f32[32,32,256]{2,1,0:T(8,128)S(1)}, u32[]{:S(2)}, u32[]{:S(2)}) async-start(f32[32,32,256]{2,1,0:T(8,128)} %bitcast.8), calls=%async_computation.1 | async-start | bytes 2097152 | tf_op jit(solution)/shard_map/all_to_all | solution.py:338
  54.2 1.3 %collective-permute-start = (f32[2,32,1024]{2,1,0:T(8,128)S(1)}, f32[2,32,1024]{2,1,0:T(8,128)S(1)}, u32[]{:S(2)}, u32[]{:S(2)}) collective-permute-start(f32[2,32,1024]{2,1,0:T(8,128)S(1)} %get-tuple-element.29), channel_id=1, source_target_pairs={{0,32},{32,64},{64,96},{96,128},{128,160},{160,192},{192,224},{1,3... | collective-permute-start | bytes 786440 | tf_op jit(solution)/shard_map/ppermute | solution.py:343
  55.5 1.3 %collective-permute-start.1 = (f32[2,32,1024]{2,1,0:T(8,128)S(1)}, f32[2,32,1024]{2,1,0:T(8,128)S(1)}, u32[]{:S(2)}, u32[]{:S(2)}) collective-permute-start(f32[2,32,1024]{2,1,0:T(8,128)S(1)} %get-tuple-element.28), channel_id=1, source_target_pairs={{32,0},{64,32},{96,64},{128,96},{160,128},{192,160},{224,192},{33,... | collective-permute-start | bytes 786440 | tf_op jit(solution)/shard_map/ppermute | solution.py:344
  56.8 3.8 %collective-permute-done.1.above_ref = f32[2,32,1024]{2,1,0:T(8,128)S(1)} collective-permute-done((f32[2,32,1024]{2,1,0:T(8,128)S(1)}, f32[2,32,1024]{2,1,0:T(8,128)S(1)}, u32[]{:S(2)}, u32[]{:S(2)}) %collective-permute-start.1) | collective-permute-done | bytes 262176 | tf_op jit(solution)/shard_map/ppermute | solution.py:344
  60.7 1.6 %copy-done.1 = bf16[1024,1024]{1,0:T(8,128)(2,1)S(1)} copy-done((bf16[1024,1024]{1,0:T(8,128)(2,1)S(1)}, bf16[1024,1024]{1,0:T(8,128)(2,1)}, u32[]{:S(2)}) %copy-start.1) | copy-done | bytes 2097176
  62.3 1.6 %copy-done.3 = bf16[1024,1024]{1,0:T(8,128)(2,1)S(1)} copy-done((bf16[1024,1024]{1,0:T(8,128)(2,1)S(1)}, bf16[1024,1024]{1,0:T(8,128)(2,1)}, u32[]{:S(2)}) %copy-start.3) | copy-done | bytes 2097176
  63.8 2.6 %first.1.bv_ref = f32[8,32,1024]{2,1,0:T(8,128)S(1)} custom-call(bf16[1024,1024]{1,0:T(8,128)(2,1)S(1)} %copy-done.1, bf16[1024,1024]{1,0:T(8,128)(2,1)S(1)} %copy-done.3, f32[8,1024]{1,0:T(8,128)S(1)} %copy-done.7, f32[6,8]{1,0:T(8,128)S(1)} %copy-done.8, f32[8,32,1024]{2,1,0:T(8,128)S(1)} %copy-done, f32[2,32,1024]{2,1,0:T(8,128)S(1)} %collective-permute-done.below_ref, ...), custom_call_target="tpu_custom_call" | custom-call | flops 1610612736 | bytes 7340032 | tf_op jit(solution)/shard_map/first/pallas_call | solution.py:216
  66.5 4.8 %second.3 = f32[1024,256]{1,0:T(8,128)} custom-call(bf16[2,1024,1024]{2,1,0:T(8,128)(2,1)} %get-tuple-element.19.both_ref, f32[8,1024]{1,0:T(8,128)} %get-tuple-element.20.exits_ref, f32[1024,256]{1,0:T(8,128)} %second.2.mass_ref), custom_call_target="tpu_custom_call" | custom-call | flops 1610612736 | bytes 6291456 | tf_op jit(solution)/shard_map/second/pallas_call | solution.py:162
  71.3 9.9 %all-to-all-done.1.w_ref = f32[32,32,256]{2,1,0:T(8,128)S(1)} async-done(((f32[32,32,256]{2,1,0:T(8,128)}), f32[32,32,256]{2,1,0:T(8,128)S(1)}, u32[]{:S(2)}, u32[]{:S(2)}) %all-to-all-start.1) | async-done | bytes 1048608 | tf_op jit(solution)/shard_map/all_to_all | solution.py:338
  81.1 5.6 %all-to-all-start.2 = ((f32[32,32,256]{2,1,0:T(8,128)}), f32[32,32,256]{2,1,0:T(8,128)}, u32[]{:S(2)}, u32[]{:S(2)}) async-start(f32[32,32,256]{2,1,0:T(8,128)} %bitcast.10), calls=%async_computation.2 | async-start | bytes 2097152 | tf_op jit(solution)/shard_map/all_to_all | solution.py:338
  86.9 1.3 %collective-permute-start.2 = (f32[2,32,1024]{2,1,0:T(8,128)S(1)}, f32[2,32,1024]{2,1,0:T(8,128)S(1)}, u32[]{:S(2)}, u32[]{:S(2)}) collective-permute-start(f32[2,32,1024]{2,1,0:T(8,128)S(1)} %get-tuple-element.23), channel_id=1, source_target_pairs={{0,32},{32,64},{64,96},{96,128},{128,160},{160,192},{192,224},{1,3... | collective-permute-start | bytes 786440 | tf_op jit(solution)/shard_map/ppermute | solution.py:343
  88.2 1.3 %collective-permute-start.3 = (f32[2,32,1024]{2,1,0:T(8,128)S(1)}, f32[2,32,1024]{2,1,0:T(8,128)S(1)}, u32[]{:S(2)}, u32[]{:S(2)}) collective-permute-start(f32[2,32,1024]{2,1,0:T(8,128)S(1)} %get-tuple-element.24), channel_id=1, source_target_pairs={{32,0},{64,32},{96,64},{128,96},{160,128},{192,160},{224,192},{33,... | collective-permute-start | bytes 786440 | tf_op jit(solution)/shard_map/ppermute | solution.py:344
  89.5 3.8 %collective-permute-done.3.above_ref = f32[2,32,1024]{2,1,0:T(8,128)S(1)} collective-permute-done((f32[2,32,1024]{2,1,0:T(8,128)S(1)}, f32[2,32,1024]{2,1,0:T(8,128)S(1)}, u32[]{:S(2)}, u32[]{:S(2)}) %collective-permute-start.3) | collective-permute-done | bytes 262176 | tf_op jit(solution)/shard_map/ppermute | solution.py:344
  93.4 1.6 %copy-done.2 = bf16[1024,1024]{1,0:T(8,128)(2,1)S(1)} copy-done((bf16[1024,1024]{1,0:T(8,128)(2,1)S(1)}, bf16[1024,1024]{1,0:T(8,128)(2,1)}, u32[]{:S(2)}) %copy-start.2) | copy-done | bytes 2097176
  95.0 1.6 %copy-done.4 = bf16[1024,1024]{1,0:T(8,128)(2,1)S(1)} copy-done((bf16[1024,1024]{1,0:T(8,128)(2,1)S(1)}, bf16[1024,1024]{1,0:T(8,128)(2,1)}, u32[]{:S(2)}) %copy-start.4) | copy-done | bytes 2097176
  96.5 2.9 %twice.1 = (f32[8,32,1024]{2,1,0:T(8,128)S(1)}, f32[8,32,1024]{2,1,0:T(8,128)S(1)}) custom-call(bf16[1024,1024]{1,0:T(8,128)(2,1)S(1)} %copy-done.2, bf16[1024,1024]{1,0:T(8,128)(2,1)S(1)} %copy-done.4, f32[8,1024]{1,0:T(8,128)S(1)} %copy-done.7, f32[6,8]{1,0:T(8,128)S(1)} %copy-done.8, f32[8,32,1024]{2,1,0:T(8,128)S(1)} %copy-done, ...), custom_call_target="tpu_custom_call" | custom-call | flops 1610612736 | bytes 9437184 | tf_op jit(solution)/shard_map/twice/pallas_call | solution.py:281
  101.4 13.1 %all-to-all-done.2.w_ref = f32[32,32,256]{2,1,0:T(8,128)} async-done(((f32[32,32,256]{2,1,0:T(8,128)}), f32[32,32,256]{2,1,0:T(8,128)}, u32[]{:S(2)}, u32[]{:S(2)}) %all-to-all-start.2) | async-done | bytes 1048608 | tf_op jit(solution)/shard_map/all_to_all | solution.py:338
  114.5 3.8 %finish.1 = (f32[8,32,1024]{2,1,0:T(8,128)}, f32[8,32,1024]{2,1,0:T(8,128)}) custom-call(f32[8,32,1024]{2,1,0:T(8,128)} %copy-done.5, f32[8,32,1024]{2,1,0:T(8,128)} %copy-done.6, f32[32,32,256]{2,1,0:T(8,128)} %all-to-all-done.2.w_ref), custom_call_target="tpu_custom_call" | custom-call | flops 1048576 | bytes 5242880 | tf_op jit(solution)/shard_map/finish/pallas_call | solution.py:318
  (20 shorter events, 3.1 us)
Async XLA Ops:
  2.9 39.8 %all-to-all-start = ((f32[32,32,256]{2,1,0:T(8,128)}), f32[32,32,256]{2,1,0:T(8,128)S(1)}, u32[]{:S(2)}, u32[]{:S(2)}) async-start(f32[32,32,256]{2,1,0:T(8,128)} %bitcast.4), calls=%async_computation | async-start | bytes 2097152 | tf_op jit(solution)/shard_map/all_to_all | solution.py:338
  42.7 1.0 copy-start.9
  43.7 10.5 %copy-start = (f32[8,32,1024]{2,1,0:T(8,128)S(1)}, f32[8,32,1024]{2,1,0:T(8,128)}, u32[]{:S(2)}) copy-start(f32[8,32,1024]{2,1,0:T(8,128)} %v_ref.3) | copy-start | bytes 3145732
  43.7 17.0 %copy-start.7 = (f32[8,1024]{1,0:T(8,128)S(1)}, f32[8,1024]{1,0:T(8,128)}, u32[]{:S(2)}) copy-start(f32[8,1024]{1,0:T(8,128)} %get-tuple-element.17.exits_ref) | copy-start | bytes 98308
  43.7 17.0 %copy-start.8 = (f32[6,8]{1,0:T(8,128)S(1)}, f32[6,8]{1,0:T(8,128)}, u32[]{:S(2)}) copy-start(f32[6,8]{1,0:T(8,128)} %get-tuple-element.18.coef_ref) | copy-start | bytes 580
  48.6 32.6 %all-to-all-start.1 = ((f32[32,32,256]{2,1,0:T(8,128)}), f32[32,32,256]{2,1,0:T(8,128)S(1)}, u32[]{:S(2)}, u32[]{:S(2)}) async-start(f32[32,32,256]{2,1,0:T(8,128)} %bitcast.8), calls=%async_computation.1 | async-start | bytes 2097152 | tf_op jit(solution)/shard_map/all_to_all | solution.py:338
  54.2 2.6 %collective-permute-start = (f32[2,32,1024]{2,1,0:T(8,128)S(1)}, f32[2,32,1024]{2,1,0:T(8,128)S(1)}, u32[]{:S(2)}, u32[]{:S(2)}) collective-permute-start(f32[2,32,1024]{2,1,0:T(8,128)S(1)} %get-tuple-element.29), channel_id=1, source_target_pairs={{0,32},{32,64},{64,96},{96,128},{128,160},{160,192},{192,224},{1,3... | collective-permute-start | bytes 786440 | tf_op jit(solution)/shard_map/ppermute | solution.py:343
  55.5 5.1 %collective-permute-start.1 = (f32[2,32,1024]{2,1,0:T(8,128)S(1)}, f32[2,32,1024]{2,1,0:T(8,128)S(1)}, u32[]{:S(2)}, u32[]{:S(2)}) collective-permute-start(f32[2,32,1024]{2,1,0:T(8,128)S(1)} %get-tuple-element.28), channel_id=1, source_target_pairs={{32,0},{64,32},{96,64},{128,96},{160,128},{192,160},{224,192},{33,... | collective-permute-start | bytes 786440 | tf_op jit(solution)/shard_map/ppermute | solution.py:344
  60.7 1.6 %copy-start.1 = (bf16[1024,1024]{1,0:T(8,128)(2,1)S(1)}, bf16[1024,1024]{1,0:T(8,128)(2,1)}, u32[]{:S(2)}) copy-start(bf16[1024,1024]{1,0:T(8,128)(2,1)} %get-tuple-element.15.high_ref) | copy-start | bytes 6291460
  62.3 1.6 %copy-start.3 = (bf16[1024,1024]{1,0:T(8,128)(2,1)S(1)}, bf16[1024,1024]{1,0:T(8,128)(2,1)}, u32[]{:S(2)}) copy-start(bf16[1024,1024]{1,0:T(8,128)(2,1)} %get-tuple-element.16.low_ref) | copy-start | bytes 6291460
  81.1 33.3 %all-to-all-start.2 = ((f32[32,32,256]{2,1,0:T(8,128)}), f32[32,32,256]{2,1,0:T(8,128)}, u32[]{:S(2)}, u32[]{:S(2)}) async-start(f32[32,32,256]{2,1,0:T(8,128)} %bitcast.10), calls=%async_computation.2 | async-start | bytes 2097152 | tf_op jit(solution)/shard_map/all_to_all | solution.py:338
  86.9 2.6 %collective-permute-start.2 = (f32[2,32,1024]{2,1,0:T(8,128)S(1)}, f32[2,32,1024]{2,1,0:T(8,128)S(1)}, u32[]{:S(2)}, u32[]{:S(2)}) collective-permute-start(f32[2,32,1024]{2,1,0:T(8,128)S(1)} %get-tuple-element.23), channel_id=1, source_target_pairs={{0,32},{32,64},{64,96},{96,128},{128,160},{160,192},{192,224},{1,3... | collective-permute-start | bytes 786440 | tf_op jit(solution)/shard_map/ppermute | solution.py:343
  88.2 5.1 %collective-permute-start.3 = (f32[2,32,1024]{2,1,0:T(8,128)S(1)}, f32[2,32,1024]{2,1,0:T(8,128)S(1)}, u32[]{:S(2)}, u32[]{:S(2)}) collective-permute-start(f32[2,32,1024]{2,1,0:T(8,128)S(1)} %get-tuple-element.24), channel_id=1, source_target_pairs={{32,0},{64,32},{96,64},{128,96},{160,128},{192,160},{224,192},{33,... | collective-permute-start | bytes 786440 | tf_op jit(solution)/shard_map/ppermute | solution.py:344
  93.4 1.6 %copy-start.2 = (bf16[1024,1024]{1,0:T(8,128)(2,1)S(1)}, bf16[1024,1024]{1,0:T(8,128)(2,1)}, u32[]{:S(2)}) copy-start(bf16[1024,1024]{1,0:T(8,128)(2,1)} %get-tuple-element.15.high_ref) | copy-start | bytes 6291460
  95.0 1.6 %copy-start.4 = (bf16[1024,1024]{1,0:T(8,128)(2,1)S(1)}, bf16[1024,1024]{1,0:T(8,128)(2,1)}, u32[]{:S(2)}) copy-start(bf16[1024,1024]{1,0:T(8,128)(2,1)} %get-tuple-element.16.low_ref) | copy-start | bytes 6291460
  99.4 1.0 copy-start.5
  100.4 1.0 copy-start.6

commit v2 on v1

--- a/solution.py
+++ b/solution.py
@@ -12,6 +12,7 @@
 LANES = 256
 SIDE = 4
 OFFSETS = (-2, -1, 1, 2)
+PLANES = 17
 HBM = pl.BlockSpec(memory_space=pltpu.HBM)
 WHOLE = pl.BlockSpec(memory_space=pltpu.VMEM)
 SCALARS = pl.BlockSpec(memory_space=pltpu.SMEM)
@@ -131,8 +132,8 @@
         ],
         out_shape=[
             half, half, jax.ShapeDtypeStruct((8, order), F32),
-            jax.ShapeDtypeStruct((2, order, order), BF16),
-            jax.ShapeDtypeStruct((8, order), F32), jax.ShapeDtypeStruct((6, levels), F32),
+            jax.ShapeDtypeStruct((PLANES, order, order), BF16),
+            jax.ShapeDtypeStruct((PLANES * order // 2, order), F32), jax.ShapeDtypeStruct((6, levels), F32),
         ],
         scratch_shapes=[pltpu.SMEM((2,), F32)],
         compiler_params=params(60),
@@ -144,6 +145,26 @@
     )
 
 
+def pack_kernel(v_ref, out_ref):
+    for p in range(out_ref.shape[1]):
+        out_ref[:, p] = v_ref[:, :, pl.ds(p * LANES, LANES)]
+
+
+def pack(v, tall=4):
+    levels, rows, order = v.shape
+    parts = order // LANES
+    return pl.pallas_call(
+        pack_kernel,
+        grid=(levels // tall,),
+        in_specs=[pl.BlockSpec((tall, rows, order), lambda i: (i, 0, 0))],
+        out_specs=pl.BlockSpec((tall, parts, rows, LANES), lambda i: (i, 0, 0, 0)),
+        out_shape=jax.ShapeDtypeStruct((levels, parts, rows, LANES), F32),
+        compiler_params=params(62),
+        cost_estimate=pl.CostEstimate(flops=0, bytes_accessed=2 << 20, transcendentals=0),
+        name="pack",
+    )(v)
+
+
 def turned_kernel(both_ref, exits_ref, mass_ref, out_ref, up, down):
     @pl.when(pl.program_id(0) == 0)
     def _():
@@ -165,12 +186,12 @@
         in_specs=[
             pl.BlockSpec((2, tall, order), lambda i: (0, i, 0)),
             pl.BlockSpec((8, tall), lambda i: (0, i)),
-            pl.BlockSpec((order, width), lambda i: (0, 0)),
+            WHOLE,
         ],
         out_specs=pl.BlockSpec((tall, width), lambda i: (i, 0)),
         out_shape=jax.ShapeDtypeStruct(mass.shape, F32),
         scratch_shapes=[pltpu.VMEM((order, width), BF16), pltpu.VMEM((order, width), BF16)],
-        compiler_params=params(60),
+        compiler_params=params(32),
         cost_estimate=pl.CostEstimate(flops=3 << 29, bytes_accessed=6 << 20, transcendentals=0),
         name="second",
     )(both, exits, mass)
@@ -246,13 +267,13 @@
         in_specs=[WHOLE, WHOLE],
         out_specs=[WHOLE, WHOLE, WHOLE],
         out_shape=[jax.ShapeDtypeStruct(bv.shape, F32), edge, edge],
-        compiler_params=params(12),
+        compiler_params=params(62),
         cost_estimate=pl.CostEstimate(flops=1 << 20, bytes_accessed=4 << 20, transcendentals=0),
         name="once",
     )(bv, w)
 
 
-def twice_kernel(high_ref, low_ref, exits_ref, coef_ref, v_ref, bv_ref, s_ref, below_ref, above_ref, step_ref, trans_ref):
+def twice_kernel(high_ref, low_ref, exits_ref, coef_ref, v_ref, bv_ref, s_ref, below_ref, above_ref, both_ref):
     levels, rows, order = v_ref.shape
     x = halves(s_ref[...].reshape(levels * rows, order))
     scale = coef_ref[5, 0]
@@ -272,63 +293,49 @@
             change = prod[m] - here * (exits_ref[0:1, cols] + coef_ref[4, m])
             stepped = here + scale * (change + hops(coef_ref, m, get, levels))
             once = 0.5 * (here + bv_ref[m, :, cols])
-            step_ref[m, :, cols] = stepped
-            trans_ref[m, :, cols] = (v_ref[m, :, cols] + once) * 0.4 + 0.2 * stepped
+            both_ref[0, m, :, cols] = stepped
+            both_ref[1, m, :, cols] = (v_ref[m, :, cols] + once) * 0.4 + 0.2 * stepped
 
 
 def twice(high, low, exits, coef, v, bv, s, below, above):
-    shape = jax.ShapeDtypeStruct(v.shape, F32)
     return pl.pallas_call(
         twice_kernel,
+        grid=(1,),
         in_specs=[WHOLE, WHOLE, WHOLE, SCALARS, WHOLE, WHOLE, WHOLE, WHOLE, WHOLE],
-        out_specs=[WHOLE, WHOLE],
-        out_shape=[shape, shape],
-        compiler_params=params(24),
+        out_specs=pl.BlockSpec((2, *v.shape), lambda i: (0, 0, 0, 0)),
+        out_shape=jax.ShapeDtypeStruct((2 * PLANES, *v.shape), F32),
+        compiler_params=params(32),
         cost_estimate=pl.CostEstimate(flops=3 << 29, bytes_accessed=9 << 20, transcendentals=0),
         name="twice",
     )(high, low, exits, coef, v, bv, s, below, above)
 
 
-def finish_kernel(step_ref, trans_ref, w_ref, out_t_ref, out_s_ref, step, trans, sems):
-    levels, _, order = step_ref.shape
+def finish_kernel(both_ref, w_ref, out_t_ref, out_s_ref):
+    levels, _, order = out_s_ref.shape
     parts = order // LANES
-    pairs = ((step_ref, step, out_s_ref), (trans_ref, trans, out_t_ref))
-    loads = [[pltpu.make_async_copy(src.at[m], buf.at[m], sems.at[m, k]) for k, (src, buf, _) in enumerate(pairs)] for m in range(levels)]
-    stores = [[pltpu.make_async_copy(buf.at[m], dst.at[m], sems.at[m, 2 + k]) for k, (_, buf, dst) in enumerate(pairs)] for m in range(levels)]
-    for group in loads:
-        for load in group:
-            load.start()
+    at = pl.program_id(0) * levels * parts
     for m in range(levels):
-        for load in loads[m]:
-            load.wait()
         for p in range(parts):
             cols = pl.ds(p * LANES, LANES)
-            more = w_ref[m * parts + p]
-            step[m, :, cols] = step[m, :, cols] + more
-            trans[m, :, cols] = trans[m, :, cols] + 0.2 * more
-        for store in stores[m]:
-            store.start()
-    for group in stores:
-        for store in group:
-            store.wait()
-
-
-def finish(step, trans, w):
-    shape = jax.ShapeDtypeStruct(step.shape, F32)
+            more = w_ref[at + m * parts + p]
+            out_s_ref[m, :, cols] = both_ref[0, m, :, cols] + more
+            out_t_ref[m, :, cols] = both_ref[1, m, :, cols] + 0.2 * more
+
+
+def finish(both, w, tall=4):
+    _, levels, rows, order = both.shape
+    shape = jax.ShapeDtypeStruct((levels, rows, order), F32)
+    block = pl.BlockSpec((tall, rows, order), lambda i: (i, 0, 0))
     return pl.pallas_call(
         finish_kernel,
-        in_specs=[HBM, HBM, WHOLE],
-        out_specs=[HBM, HBM],
+        grid=(levels // tall,),
+        in_specs=[pl.BlockSpec((2, tall, rows, order), lambda i: (0, i, 0, 0)), WHOLE],
+        out_specs=[block, block],
         out_shape=[shape, shape],
-        scratch_shapes=[
-            pltpu.VMEM(step.shape, F32),
-            pltpu.VMEM(step.shape, F32),
-            pltpu.SemaphoreType.DMA((step.shape[0], 4)),
-        ],
-        compiler_params=params(60),
+        compiler_params=params(32),
         cost_estimate=pl.CostEstimate(flops=1 << 20, bytes_accessed=5 << 20, transcendentals=0),
         name="finish",
-    )(step, trans, w)
+    )(both, w)
 
 
 def swap(chunks):
@@ -348,25 +355,26 @@
 def local(initial, rates_first, blocks_first, rates_second, blocks_second, level_rate, level_code):
     levels, rows, order = initial.shape
     count = lax.axis_size("comp")
-    turned_mass = swap(initial.reshape(levels, rows, order // LANES, LANES).transpose(0, 2, 1, 3).reshape(count, rows, LANES)).reshape(order, LANES)
+    turned_mass = swap(pack(initial).reshape(count, rows, LANES)).reshape(order, LANES)
 
     below, above = neighbours(initial[:2], initial[levels - 2 :])
     start = (lax.axis_index("ctr") * levels).astype(jnp.int32).reshape(1)
     fst_high, fst_low, exits, sec_both, sec_exits, coef = prepare(
         level_rate, level_code, start, rates_first, blocks_first, rates_second, blocks_second, levels, count
     )
-    bv = first(fst_high, fst_low, exits, coef, initial, below, above)
-
+
+    turned_mass, below, above = lax.optimization_barrier((turned_mass, below, above))
     w_one = turned(sec_both, sec_exits, turned_mass)
     back_one = swap(w_one.reshape(count, rows, LANES))
+    bv = first(fst_high, fst_low, exits, coef, initial, below, above)
     w_two = turned(sec_both, sec_exits, w_one)
     w_two, bv = lax.optimization_barrier((w_two, bv))
     back_two = swap(w_two.reshape(count, rows, LANES))
 
     s, low, top = gather(bv, back_one)
     s_below, s_above = neighbours(low, top)
-    step, trans = twice(fst_high, fst_low, exits, coef, initial, bv, s, s_below, s_above)
-    transient, stepped = finish(step, trans, back_two)
+    both = twice(fst_high, fst_low, exits, coef, initial, bv, s, s_below, s_above)
+    transient, stepped = finish(both, back_two)
     return transient, stepped
 
 

time: 119 us -> 116 us (0.975)
  Pallas kernels: 28.8 us -> 33.7 us
  local copies, waits for them, and re-layouts: 10.6 us -> 6.65 us
  waiting for transfers between devices: 49 us -> 45.6 us
    ppermute x2, waiting for transfers between devices: 7.66 us -> 4.02 us  [neighbours(): above = lax.ppermute(low, 'ctr', [(i + 1, i) for i in range(count - 1)])]
    unnamed x20, local copies, waits for them, and re-layouts: 9.3 us -> 6.62 us
    pallas_call x1, Pallas kernels: 0.12 us -> 2.71 us  [gather(): pl.pallas_call(gather_kernel, in_specs=[WHOLE, WHOLE], out_specs=[WHOLE,...]
    pallas_call x2 -> x3, Pallas kernels: 6.74 us -> 9.26 us  [the longest x1 4.18 us: twice(): pl.pallas_call(twice_kernel, grid=(1,), in_specs=[WHOLE, WHOLE, WHOLE, SC...]
    slice x1 -> x0, local copies, waits for them, and re-layouts: 1.27 us -> none
  transfers between devices with their start and end apart: 7 -> 7, of which waited for: 5 -> 4; matrix products, arithmetic and copies ran while one was open for 0% -> 0% of each run, Pallas kernels for 17% -> 21%
where the time goes in v2:
time: 116 us; the launch traced here: 115 us
  waiting for transfers between devices  45.6 us (39%)
  Pallas kernels  33.7 us (29%)
  starting transfers between devices  28.1 us (24%)
  local copies, waits for them, and re-layouts  6.65 us (6%)
    all_to_all x3, waiting for transfers between devices, swap(): lax.all_to_all(chunks, 'comp', split_axis=0, concat_axis=0, axis_index_gr...  41.6 us
    all_to_all x3, starting transfers between devices, swap(): lax.all_to_all(chunks, 'comp', split_axis=0, concat_axis=0, axis_index_gr...  22.9 us
    pallas_call x1, Pallas kernels, prepare(): pl.pallas_call(prepare_kernel, grid=(order // tall,), in_specs=[SCALARS,...  9.61 us
    pallas_call x2, Pallas kernels, turned(): pl.pallas_call(turned_kernel, grid=(order // tall,), in_specs=[pl.BlockSp...  9.47 us
    unnamed x20, local copies, waits for them, and re-layouts  6.62 us
    pallas_call x1, Pallas kernels, twice(): pl.pallas_call(twice_kernel, grid=(1,), in_specs=[WHOLE, WHOLE, WHOLE, SC...  4.18 us
    ppermute x2, waiting for transfers between devices, neighbours(): above = lax.ppermute(low, 'ctr', [(i + 1, i) for i in range(count - 1)])  4.02 us
    pallas_call x1, Pallas kernels, finish(): pl.pallas_call(finish_kernel, grid=(levels // tall,), in_specs=[pl.BlockS...  2.94 us
  transfers between devices with their start and end apart: 7, of which 4 were waited for; matrix products, arithmetic and copies ran while one was open for 0% of the time, Pallas kernels for 21%

profile of v2, /device:TPU:8, one launch (start us, length us, event | category | flops | bytes accessed | tf_op | source)
XLA Modules:
  0.0 114.9 jit_solution(8023158942172720761)
XLA Ops:
  0.6 2.1 %pack.1 = f32[8,4,32,256]{3,2,1,0:T(8,128)} custom-call(f32[8,32,1024]{2,1,0:T(8,128)} %v_ref.5), custom_call_target="tpu_custom_call" | custom-call | bytes 2097152 | tf_op jit(solution)/shard_map/pack/pallas_call | solution.py:156
  2.8 11.7 %all-to-all-start = ((f32[32,32,256]{2,1,0:T(8,128)}), f32[32,32,256]{2,1,0:T(8,128)S(1)}, u32[]{:S(2)}, u32[]{:S(2)}) async-start(f32[32,32,256]{2,1,0:T(8,128)} %bitcast.10), calls=%async_computation | async-start | bytes 2097152 | tf_op jit(solution)/shard_map/all_to_all | solution.py:345
  14.5 1.3 %collective-permute-start = (f32[2,32,1024]{2,1,0:T(8,128)S(1)}, f32[2,32,1024]{2,1,0:T(8,128)S(1)}, u32[]{:S(2)}, u32[]{:S(2)}) collective-permute-start(f32[2,32,1024]{2,1,0:T(8,128)S(1)} %get-tuple-element.31), channel_id=1, source_target_pairs={{0,32},{32,64},{64,96},{96,128},{128,160},{160,192},{192,224},{1,3... | collective-permute-start | bytes 786440 | tf_op jit(solution)/shard_map/ppermute | solution.py:350
  15.9 1.3 %collective-permute-start.1 = (f32[2,32,1024]{2,1,0:T(8,128)S(1)}, f32[2,32,1024]{2,1,0:T(8,128)S(1)}, u32[]{:S(2)}, u32[]{:S(2)}) collective-permute-start(f32[2,32,1024]{2,1,0:T(8,128)S(1)} %get-tuple-element.30), channel_id=1, source_target_pairs={{32,0},{64,32},{96,64},{128,96},{160,128},{192,160},{224,192},{33,... | collective-permute-start | bytes 786440 | tf_op jit(solution)/shard_map/ppermute | solution.py:351
  17.2 9.6 %prepare.1 = (bf16[1024,1024]{1,0:T(8,128)(2,1)}, bf16[1024,1024]{1,0:T(8,128)(2,1)}, f32[8,1024]{1,0:T(8,128)}, bf16[17,1024,1024]{2,1,0:T(8,128)(2,1)}, f32[8704,1024]{1,0:T(8,128)}, /*index=5*/f32[6,8]{1,0:T(8,128)}) custom-call(f32[64]{0:T(128)} %rate_ref.1, s32[64]{0:T(128)} %code_ref.1, s32[1]{0:T(128)} %bitcast.start_ref, f32[1,64]{1,0:T(1,128)} %bitcast.11, ...), custom_call_target="tpu_custom_call" | custom-call | flops 134217728 | bytes 16777216 | tf_op jit(solution)/shard_map/prepare/pallas_call | solution.py:125
  26.8 15.8 %all-to-all-done = f32[32,32,256]{2,1,0:T(8,128)S(1)} async-done(((f32[32,32,256]{2,1,0:T(8,128)}), f32[32,32,256]{2,1,0:T(8,128)S(1)}, u32[]{:S(2)}, u32[]{:S(2)}) %all-to-all-start) | async-done | bytes 1048608 | tf_op jit(solution)/shard_map/all_to_all | solution.py:345
  42.6 4.5 %second.2.mass_ref = f32[1024,256]{1,0:T(8,128)} custom-call(bf16[17,1024,1024]{2,1,0:T(8,128)(2,1)} %get-tuple-element.20.both_ref, f32[8704,1024]{1,0:T(8,128)} %get-tuple-element.21.exits_ref, f32[1024,256]{1,0:T(8,128)S(1)} %bitcast.8), custom_call_target="tpu_custom_call" | custom-call | flops 1610612736 | bytes 6291456 | tf_op jit(solution)/shard_map/second/pallas_call | solution.py:183
  47.1 5.6 %all-to-all-start.1 = ((f32[32,32,256]{2,1,0:T(8,128)}), f32[32,32,256]{2,1,0:T(8,128)}, u32[]{:S(2)}, u32[]{:S(2)}) async-start(f32[32,32,256]{2,1,0:T(8,128)} %bitcast.6), calls=%async_computation.1 | async-start | bytes 2097152 | tf_op jit(solution)/shard_map/all_to_all | solution.py:345
  52.7 5.0 %second.3 = f32[1024,256]{1,0:T(8,128)} custom-call(bf16[17,1024,1024]{2,1,0:T(8,128)(2,1)} %get-tuple-element.20.both_ref, f32[8704,1024]{1,0:T(8,128)} %get-tuple-element.21.exits_ref, f32[1024,256]{1,0:T(8,128)} %second.2.mass_ref), custom_call_target="tpu_custom_call" | custom-call | flops 1610612736 | bytes 6291456 | tf_op jit(solution)/shard_map/second/pallas_call | solution.py:183
  57.7 2.6 %first.1.bv_ref = f32[8,32,1024]{2,1,0:T(8,128)S(1)} custom-call(bf16[1024,1024]{1,0:T(8,128)(2,1)S(1)} %copy-done.3, bf16[1024,1024]{1,0:T(8,128)(2,1)S(1)} %copy-done.5, f32[8,1024]{1,0:T(8,128)S(1)} %copy-done.8, f32[6,8]{1,0:T(8,128)S(1)} %copy-done.9, f32[8,32,1024]{2,1,0:T(8,128)S(1)} %copy-done, f32[2,32,1024]{2,1,0:T(8,128)S(1)} %collective-permute-done.below_ref, ...), custom_call_target="tpu_custom_call" | custom-call | flops 1610612736 | bytes 7340032 | tf_op jit(solution)/shard_map/first/pallas_call | solution.py:237
  60.4 1.0 copy-done.1
  61.3 18.4 %all-to-all-done.1.w_ref = f32[32,32,256]{2,1,0:T(8,128)} async-done(((f32[32,32,256]{2,1,0:T(8,128)}), f32[32,32,256]{2,1,0:T(8,128)}, u32[]{:S(2)}, u32[]{:S(2)}) %all-to-all-start.1) | async-done | bytes 1048608 | tf_op jit(solution)/shard_map/all_to_all | solution.py:345
  79.7 5.6 %all-to-all-start.2 = ((f32[32,32,256]{2,1,0:T(8,128)}), f32[32,32,256]{2,1,0:T(8,128)}, u32[]{:S(2)}, u32[]{:S(2)}) async-start(f32[32,32,256]{2,1,0:T(8,128)} %bitcast.7), calls=%async_computation.2 | async-start | bytes 2097152 | tf_op jit(solution)/shard_map/all_to_all | solution.py:345
  85.4 2.7 %once.1 = (f32[8,32,1024]{2,1,0:T(8,128)}, f32[2,32,1024]{2,1,0:T(8,128)}, f32[2,32,1024]{2,1,0:T(8,128)}) custom-call(f32[8,32,1024]{2,1,0:T(8,128)} %copy-done.1, f32[32,32,256]{2,1,0:T(8,128)} %all-to-all-done.1.w_ref), custom_call_target="tpu_custom_call" | custom-call | flops 1048576 | bytes 4194304 | tf_op jit(solution)/shard_map/once/pallas_call | solution.py:265
  88.1 1.3 %collective-permute-start.2 = (f32[2,32,1024]{2,1,0:T(8,128)}, f32[2,32,1024]{2,1,0:T(8,128)S(1)}, u32[]{:S(2)}, u32[]{:S(2)}) collective-permute-start(f32[2,32,1024]{2,1,0:T(8,128)} %get-tuple-element.27), channel_id=1, source_target_pairs={{0,32},{32,64},{64,96},{96,128},{128,160},{160,192},{192,224},{1,3... | collective-permute-start | bytes 786440 | tf_op jit(solution)/shard_map/ppermute | solution.py:350
  89.4 1.3 %collective-permute-start.3 = (f32[2,32,1024]{2,1,0:T(8,128)}, f32[2,32,1024]{2,1,0:T(8,128)S(1)}, u32[]{:S(2)}, u32[]{:S(2)}) collective-permute-start(f32[2,32,1024]{2,1,0:T(8,128)} %get-tuple-element.28), channel_id=1, source_target_pairs={{32,0},{64,32},{96,64},{128,96},{160,128},{192,160},{224,192},{33,... | collective-permute-start | bytes 786440 | tf_op jit(solution)/shard_map/ppermute | solution.py:351
  90.7 4.0 %collective-permute-done.3.above_ref = f32[2,32,1024]{2,1,0:T(8,128)S(1)} collective-permute-done((f32[2,32,1024]{2,1,0:T(8,128)}, f32[2,32,1024]{2,1,0:T(8,128)S(1)}, u32[]{:S(2)}, u32[]{:S(2)}) %collective-permute-start.3) | collective-permute-done | bytes 262176 | tf_op jit(solution)/shard_map/ppermute | solution.py:351
  94.7 1.2 %copy-done.2 = f32[8,32,1024]{2,1,0:T(8,128)S(1)} copy-done((f32[8,32,1024]{2,1,0:T(8,128)S(1)}, f32[8,32,1024]{2,1,0:T(8,128)}, u32[]{:S(2)}) %copy-start.2) | copy-done | bytes 1048600
  96.0 1.6 %copy-done.4 = bf16[1024,1024]{1,0:T(8,128)(2,1)S(1)} copy-done((bf16[1024,1024]{1,0:T(8,128)(2,1)S(1)}, bf16[1024,1024]{1,0:T(8,128)(2,1)}, u32[]{:S(2)}) %copy-start.4) | copy-done | bytes 2097176
  97.6 1.6 %copy-done.6 = bf16[1024,1024]{1,0:T(8,128)(2,1)S(1)} copy-done((bf16[1024,1024]{1,0:T(8,128)(2,1)S(1)}, bf16[1024,1024]{1,0:T(8,128)(2,1)}, u32[]{:S(2)}) %copy-start.6) | copy-done | bytes 2097176
  99.1 1.2 %copy-done.7 = f32[8,32,1024]{2,1,0:T(8,128)S(1)} copy-done((f32[8,32,1024]{2,1,0:T(8,128)S(1)}, f32[8,32,1024]{2,1,0:T(8,128)}, u32[]{:S(2)}) %copy-start.7) | copy-done | bytes 1048600
  100.4 4.2 %twice.1.both_ref = f32[34,8,32,1024]{3,2,1,0:T(8,128)} custom-call(bf16[1024,1024]{1,0:T(8,128)(2,1)S(1)} %copy-done.4, bf16[1024,1024]{1,0:T(8,128)(2,1)S(1)} %copy-done.6, f32[8,1024]{1,0:T(8,128)S(1)} %copy-done.8, f32[6,8]{1,0:T(8,128)S(1)} %copy-done.9, f32[8,32,1024]{2,1,0:T(8,128)S(1)} %copy-done, f32[8,32,1024]{2,1,0:T(8,128)S(1)} %copy-done.2, ...), custom_call_target="tpu_custom_call" | custom-call | flops 1610612736 | bytes 9437184 | tf_op jit(solution)/shard_map/twice/pallas_call | solution.py:301
  104.6 7.4 %all-to-all-done.2.w_ref = f32[32,32,256]{2,1,0:T(8,128)} async-done(((f32[32,32,256]{2,1,0:T(8,128)}), f32[32,32,256]{2,1,0:T(8,128)}, u32[]{:S(2)}, u32[]{:S(2)}) %all-to-all-start.2) | async-done | bytes 1048608 | tf_op jit(solution)/shard_map/all_to_all | solution.py:345
  112.0 2.9 %finish.1 = (f32[8,32,1024]{2,1,0:T(8,128)}, f32[8,32,1024]{2,1,0:T(8,128)}) custom-call(f32[34,8,32,1024]{3,2,1,0:T(8,128)} %twice.1.both_ref, f32[32,32,256]{2,1,0:T(8,128)} %all-to-all-done.2.w_ref), custom_call_target="tpu_custom_call" | custom-call | flops 1048576 | bytes 5242880 | tf_op jit(solution)/shard_map/finish/pallas_call | solution.py:329
  (19 shorter events, 0.1 us)
Async XLA Ops:
  0.6 13.9 %copy-start = (f32[8,32,1024]{2,1,0:T(8,128)S(1)}, f32[8,32,1024]{2,1,0:T(8,128)}, u32[]{:S(2)}) copy-start(f32[8,32,1024]{2,1,0:T(8,128)} %v_ref.5) | copy-start | bytes 3145732
  2.8 39.8 %all-to-all-start = ((f32[32,32,256]{2,1,0:T(8,128)}), f32[32,32,256]{2,1,0:T(8,128)S(1)}, u32[]{:S(2)}, u32[]{:S(2)}) async-start(f32[32,32,256]{2,1,0:T(8,128)} %bitcast.10), calls=%async_computation | async-start | bytes 2097152 | tf_op jit(solution)/shard_map/all_to_all | solution.py:345
  14.5 12.2 %collective-permute-start = (f32[2,32,1024]{2,1,0:T(8,128)S(1)}, f32[2,32,1024]{2,1,0:T(8,128)S(1)}, u32[]{:S(2)}, u32[]{:S(2)}) collective-permute-start(f32[2,32,1024]{2,1,0:T(8,128)S(1)} %get-tuple-element.31), channel_id=1, source_target_pairs={{0,32},{32,64},{64,96},{96,128},{128,160},{160,192},{192,224},{1,3... | collective-permute-start | bytes 786440 | tf_op jit(solution)/shard_map/ppermute | solution.py:350
  15.9 10.9 %collective-permute-start.1 = (f32[2,32,1024]{2,1,0:T(8,128)S(1)}, f32[2,32,1024]{2,1,0:T(8,128)S(1)}, u32[]{:S(2)}, u32[]{:S(2)}) collective-permute-start(f32[2,32,1024]{2,1,0:T(8,128)S(1)} %get-tuple-element.30), channel_id=1, source_target_pairs={{32,0},{64,32},{96,64},{128,96},{160,128},{192,160},{224,192},{33,... | collective-permute-start | bytes 786440 | tf_op jit(solution)/shard_map/ppermute | solution.py:351
  47.1 32.7 %all-to-all-start.1 = ((f32[32,32,256]{2,1,0:T(8,128)}), f32[32,32,256]{2,1,0:T(8,128)}, u32[]{:S(2)}, u32[]{:S(2)}) async-start(f32[32,32,256]{2,1,0:T(8,128)} %bitcast.6), calls=%async_computation.1 | async-start | bytes 2097152 | tf_op jit(solution)/shard_map/all_to_all | solution.py:345
  52.7 5.0 %copy-start.3 = (bf16[1024,1024]{1,0:T(8,128)(2,1)S(1)}, bf16[1024,1024]{1,0:T(8,128)(2,1)}, u32[]{:S(2)}) copy-start(bf16[1024,1024]{1,0:T(8,128)(2,1)} %get-tuple-element.16.high_ref) | copy-start | bytes 6291460
  52.7 5.0 %copy-start.5 = (bf16[1024,1024]{1,0:T(8,128)(2,1)S(1)}, bf16[1024,1024]{1,0:T(8,128)(2,1)}, u32[]{:S(2)}) copy-start(bf16[1024,1024]{1,0:T(8,128)(2,1)} %get-tuple-element.17.low_ref) | copy-start | bytes 6291460
  52.7 5.0 %copy-start.8 = (f32[8,1024]{1,0:T(8,128)S(1)}, f32[8,1024]{1,0:T(8,128)}, u32[]{:S(2)}) copy-start(f32[8,1024]{1,0:T(8,128)} %get-tuple-element.18.exits_ref) | copy-start | bytes 98308
  52.7 5.0 %copy-start.9 = (f32[6,8]{1,0:T(8,128)S(1)}, f32[6,8]{1,0:T(8,128)}, u32[]{:S(2)}) copy-start(f32[6,8]{1,0:T(8,128)} %get-tuple-element.19.coef_ref) | copy-start | bytes 580
  60.3 1.0 copy-start.1
  79.7 32.2 %all-to-all-start.2 = ((f32[32,32,256]{2,1,0:T(8,128)}), f32[32,32,256]{2,1,0:T(8,128)}, u32[]{:S(2)}, u32[]{:S(2)}) async-start(f32[32,32,256]{2,1,0:T(8,128)} %bitcast.7), calls=%async_computation.2 | async-start | bytes 2097152 | tf_op jit(solution)/shard_map/all_to_all | solution.py:345
  88.1 2.6 %collective-permute-start.2 = (f32[2,32,1024]{2,1,0:T(8,128)}, f32[2,32,1024]{2,1,0:T(8,128)S(1)}, u32[]{:S(2)}, u32[]{:S(2)}) collective-permute-start(f32[2,32,1024]{2,1,0:T(8,128)} %get-tuple-element.27), channel_id=1, source_target_pairs={{0,32},{32,64},{64,96},{96,128},{128,160},{160,192},{192,224},{1,3... | collective-permute-start | bytes 786440 | tf_op jit(solution)/shard_map/ppermute | solution.py:350
  89.4 5.4 %collective-permute-start.3 = (f32[2,32,1024]{2,1,0:T(8,128)}, f32[2,32,1024]{2,1,0:T(8,128)S(1)}, u32[]{:S(2)}, u32[]{:S(2)}) collective-permute-start(f32[2,32,1024]{2,1,0:T(8,128)} %get-tuple-element.28), channel_id=1, source_target_pairs={{32,0},{64,32},{96,64},{128,96},{160,128},{192,160},{224,192},{33,... | collective-permute-start | bytes 786440 | tf_op jit(solution)/shard_map/ppermute | solution.py:351
  94.7 1.2 %copy-start.2 = (f32[8,32,1024]{2,1,0:T(8,128)S(1)}, f32[8,32,1024]{2,1,0:T(8,128)}, u32[]{:S(2)}) copy-start(f32[8,32,1024]{2,1,0:T(8,128)} %copy-done.1) | copy-start | bytes 3145732
  96.0 1.6 %copy-start.4 = (bf16[1024,1024]{1,0:T(8,128)(2,1)S(1)}, bf16[1024,1024]{1,0:T(8,128)(2,1)}, u32[]{:S(2)}) copy-start(bf16[1024,1024]{1,0:T(8,128)(2,1)} %get-tuple-element.16.high_ref) | copy-start | bytes 6291460
  97.6 1.6 %copy-start.6 = (bf16[1024,1024]{1,0:T(8,128)(2,1)S(1)}, bf16[1024,1024]{1,0:T(8,128)(2,1)}, u32[]{:S(2)}) copy-start(bf16[1024,1024]{1,0:T(8,128)(2,1)} %get-tuple-element.17.low_ref) | copy-start | bytes 6291460
  99.1 1.2 %copy-start.7 = (f32[8,32,1024]{2,1,0:T(8,128)S(1)}, f32[8,32,1024]{2,1,0:T(8,128)}, u32[]{:S(2)}) copy-start(f32[8,32,1024]{2,1,0:T(8,128)} %get-tuple-element.26.s_ref) | copy-start | bytes 3145732

commit v3 on v2

--- a/solution.py
+++ b/solution.py
@@ -236,17 +236,18 @@
 def first(high, low, exits, coef, v, below, above):
     return pl.pallas_call(
         first_kernel,
+        grid=(1,),
         in_specs=[WHOLE, WHOLE, WHOLE, SCALARS, WHOLE, WHOLE, WHOLE],
-        out_specs=WHOLE,
-        out_shape=jax.ShapeDtypeStruct(v.shape, F32),
-        compiler_params=params(20),
+        out_specs=pl.BlockSpec(v.shape, lambda i: (0, 0, 0)),
+        out_shape=jax.ShapeDtypeStruct((2 * PLANES * v.shape[0], *v.shape[1:]), F32),
+        compiler_params=params(32),
         cost_estimate=pl.CostEstimate(flops=3 << 29, bytes_accessed=7 << 20, transcendentals=0),
         name="first",
     )(high, low, exits, coef, v, below, above)
 
 
 def gather_kernel(bv_ref, w_ref, sum_ref, low_ref, top_ref):
-    levels, _, order = bv_ref.shape
+    levels, _, order = sum_ref.shape
     parts = order // LANES
     for m in range(levels):
         for p in range(parts):
@@ -259,15 +260,17 @@
                 top_ref[m - levels + 2, :, cols] = s
 
 
-def gather(bv, w):
-    levels, rows, order = bv.shape
+def gather(bv, w, levels):
+    _, rows, order = bv.shape
+    whole = (levels, rows, order)
     edge = jax.ShapeDtypeStruct((2, rows, order), F32)
     return pl.pallas_call(
         gather_kernel,
-        in_specs=[WHOLE, WHOLE],
+        grid=(1,),
+        in_specs=[pl.BlockSpec(whole, lambda i: (0, 0, 0)), WHOLE],
         out_specs=[WHOLE, WHOLE, WHOLE],
-        out_shape=[jax.ShapeDtypeStruct(bv.shape, F32), edge, edge],
-        compiler_params=params(62),
+        out_shape=[jax.ShapeDtypeStruct(whole, F32), edge, edge],
+        compiler_params=params(32),
         cost_estimate=pl.CostEstimate(flops=1 << 20, bytes_accessed=4 << 20, transcendentals=0),
         name="once",
     )(bv, w)
@@ -301,7 +304,7 @@
     return pl.pallas_call(
         twice_kernel,
         grid=(1,),
-        in_specs=[WHOLE, WHOLE, WHOLE, SCALARS, WHOLE, WHOLE, WHOLE, WHOLE, WHOLE],
+        in_specs=[WHOLE, WHOLE, WHOLE, SCALARS, WHOLE, pl.BlockSpec(v.shape, lambda i: (0, 0, 0)), WHOLE, WHOLE, WHOLE],
         out_specs=pl.BlockSpec((2, *v.shape), lambda i: (0, 0, 0, 0)),
         out_shape=jax.ShapeDtypeStruct((2 * PLANES, *v.shape), F32),
         compiler_params=params(32),
@@ -313,11 +316,10 @@
 def finish_kernel(both_ref, w_ref, out_t_ref, out_s_ref):
     levels, _, order = out_s_ref.shape
     parts = order // LANES
-    at = pl.program_id(0) * levels * parts
     for m in range(levels):
         for p in range(parts):
             cols = pl.ds(p * LANES, LANES)
-            more = w_ref[at + m * parts + p]
+            more = w_ref[m * parts + p]
             out_s_ref[m, :, cols] = both_ref[0, m, :, cols] + more
             out_t_ref[m, :, cols] = both_ref[1, m, :, cols] + 0.2 * more
 
@@ -329,7 +331,10 @@
     return pl.pallas_call(
         finish_kernel,
         grid=(levels // tall,),
-        in_specs=[pl.BlockSpec((2, tall, rows, order), lambda i: (0, i, 0, 0)), WHOLE],
+        in_specs=[
+            pl.BlockSpec((2, tall, rows, order), lambda i: (0, i, 0, 0)),
+            pl.BlockSpec((tall * (order // LANES), rows, LANES), lambda i: (i, 0, 0)),
+        ],
         out_specs=[block, block],
         out_shape=[shape, shape],
         compiler_params=params(32),
@@ -371,7 +376,7 @@
     w_two, bv = lax.optimization_barrier((w_two, bv))
     back_two = swap(w_two.reshape(count, rows, LANES))
 
-    s, low, top = gather(bv, back_one)
+    s, low, top = gather(bv, back_one, levels)
     s_below, s_above = neighbours(low, top)
     both = twice(fst_high, fst_low, exits, coef, initial, bv, s, s_below, s_above)
     transient, stepped = finish(both, back_two)

time: 116 us -> 115 us (level)
  waiting for transfers between devices: 45.6 us -> 50.2 us
  local copies, waits for them, and re-layouts: 6.65 us -> 2.07 us
    unnamed x20 -> x18, local copies, waits for them, and re-layouts: 6.62 us -> 1 us
    all_to_all x3, waiting for transfers between devices: 41.6 us -> 46.4 us  [swap(): lax.all_to_all(chunks, 'comp', split_axis=0, concat_axis=0, axis_index_gr...]
  transfers between devices with their start and end apart: 7 -> 7, of which waited for: 4 -> 4; matrix products, arithmetic and copies ran while one was open for 0% -> 1% of each run, Pallas kernels for 21% -> 21%
where the time goes in v3:
time: 115 us
  waiting for transfers between devices  50.2 us (44%)
  Pallas kernels  33.5 us (29%)
  starting transfers between devices  28.1 us (24%)
  local copies, waits for them, and re-layouts  2.07 us (2%)
    all_to_all x3, waiting for transfers between devices, swap(): lax.all_to_all(chunks, 'comp', split_axis=0, concat_axis=0, axis_index_gr...  46.4 us
    all_to_all x3, starting transfers between devices, swap(): lax.all_to_all(chunks, 'comp', split_axis=0, concat_axis=0, axis_index_gr...  22.9 us
    pallas_call x1, Pallas kernels, prepare(): pl.pallas_call(prepare_kernel, grid=(order // tall,), in_specs=[SCALARS,...  9.58 us
    pallas_call x2, Pallas kernels, turned(): pl.pallas_call(turned_kernel, grid=(order // tall,), in_specs=[pl.BlockSp...  8.69 us
    pallas_call x1, Pallas kernels, twice(): pl.pallas_call(twice_kernel, grid=(1,), in_specs=[WHOLE, WHOLE, WHOLE, SC...  4.88 us
    ppermute x2, waiting for transfers between devices, neighbours(): above = lax.ppermute(low, 'ctr', [(i + 1, i) for i in range(count - 1)])  3.83 us
    pallas_call x1, Pallas kernels, first(): pl.pallas_call(first_kernel, grid=(1,), in_specs=[WHOLE, WHOLE, WHOLE, SC...  3.61 us
    pallas_call x1, Pallas kernels, finish(): pl.pallas_call(finish_kernel, grid=(levels // tall,), in_specs=[pl.BlockS...  2.89 us
  transfers between devices with their start and end apart: 7, of which 4 were waited for; matrix products, arithmetic and copies ran while one was open for 1% of the time, Pallas kernels for 21%

profile of v3, /device:TPU:8, one launch (start us, length us, event | category | flops | bytes accessed | tf_op | source)
XLA Modules:
  0.0 114.8 jit_solution(7285949767107996570)
XLA Ops:
  0.6 2.1 %pack.1 = f32[8,4,32,256]{3,2,1,0:T(8,128)} custom-call(f32[8,32,1024]{2,1,0:T(8,128)} %v_ref.5), custom_call_target="tpu_custom_call" | custom-call | bytes 2097152 | tf_op jit(solution)/shard_map/pack/pallas_call | solution.py:156
  2.7 11.7 %all-to-all-start = ((f32[32,32,256]{2,1,0:T(8,128)}), f32[32,32,256]{2,1,0:T(8,128)S(1)}, u32[]{:S(2)}, u32[]{:S(2)}) async-start(f32[32,32,256]{2,1,0:T(8,128)} %bitcast.11), calls=%async_computation | async-start | bytes 2097152 | tf_op jit(solution)/shard_map/all_to_all | solution.py:350
  14.4 1.1 fusion
  15.5 1.3 %collective-permute-start = (f32[2,32,1024]{2,1,0:T(8,128)S(1)}, f32[2,32,1024]{2,1,0:T(8,128)S(1)}, u32[]{:S(2)}, u32[]{:S(2)}) collective-permute-start(f32[2,32,1024]{2,1,0:T(8,128)S(1)} %get-tuple-element.31), channel_id=1, source_target_pairs={{0,32},{32,64},{64,96},{96,128},{128,160},{160,192},{192,224},{1,3... | collective-permute-start | bytes 786440 | tf_op jit(solution)/shard_map/ppermute | solution.py:355
  16.8 1.3 %collective-permute-start.1 = (f32[2,32,1024]{2,1,0:T(8,128)S(1)}, f32[2,32,1024]{2,1,0:T(8,128)S(1)}, u32[]{:S(2)}, u32[]{:S(2)}) collective-permute-start(f32[2,32,1024]{2,1,0:T(8,128)S(1)} %get-tuple-element.30), channel_id=1, source_target_pairs={{32,0},{64,32},{96,64},{128,96},{160,128},{192,160},{224,192},{33,... | collective-permute-start | bytes 786440 | tf_op jit(solution)/shard_map/ppermute | solution.py:356
  18.1 9.6 %prepare.1 = (bf16[1024,1024]{1,0:T(8,128)(2,1)}, bf16[1024,1024]{1,0:T(8,128)(2,1)}, f32[8,1024]{1,0:T(8,128)}, bf16[17,1024,1024]{2,1,0:T(8,128)(2,1)}, f32[8704,1024]{1,0:T(8,128)}, /*index=5*/f32[6,8]{1,0:T(8,128)}) custom-call(f32[64]{0:T(128)} %rate_ref.1, s32[64]{0:T(128)} %code_ref.1, s32[1]{0:T(128)} %bitcast.start_ref, f32[1,64]{1,0:T(1,128)} %bitcast.12, ...), custom_call_target="tpu_custom_call" | custom-call | flops 134217728 | bytes 16777216 | tf_op jit(solution)/shard_map/prepare/pallas_call | solution.py:125
  27.7 14.8 %all-to-all-done = f32[32,32,256]{2,1,0:T(8,128)S(1)} async-done(((f32[32,32,256]{2,1,0:T(8,128)}), f32[32,32,256]{2,1,0:T(8,128)S(1)}, u32[]{:S(2)}, u32[]{:S(2)}) %all-to-all-start) | async-done | bytes 1048608 | tf_op jit(solution)/shard_map/all_to_all | solution.py:350
  42.5 4.5 %second.2.mass_ref = f32[1024,256]{1,0:T(8,128)} custom-call(bf16[17,1024,1024]{2,1,0:T(8,128)(2,1)} %get-tuple-element.20.both_ref, f32[8704,1024]{1,0:T(8,128)} %get-tuple-element.21.exits_ref, f32[1024,256]{1,0:T(8,128)S(1)} %bitcast.8), custom_call_target="tpu_custom_call" | custom-call | flops 1610612736 | bytes 6291456 | tf_op jit(solution)/shard_map/second/pallas_call | solution.py:183
  47.0 5.6 %all-to-all-start.1 = ((f32[32,32,256]{2,1,0:T(8,128)}), f32[32,32,256]{2,1,0:T(8,128)}, u32[]{:S(2)}, u32[]{:S(2)}) async-start(f32[32,32,256]{2,1,0:T(8,128)} %bitcast.6), calls=%async_computation.1 | async-start | bytes 2097152 | tf_op jit(solution)/shard_map/all_to_all | solution.py:350
  52.6 0.0 copy-start
  52.7 4.2 %second.3 = f32[1024,256]{1,0:T(8,128)S(1)} custom-call(bf16[17,1024,1024]{2,1,0:T(8,128)(2,1)} %get-tuple-element.20.both_ref, f32[8704,1024]{1,0:T(8,128)} %get-tuple-element.21.exits_ref, f32[1024,256]{1,0:T(8,128)} %second.2.mass_ref), custom_call_target="tpu_custom_call" | custom-call | flops 1610612736 | bytes 6291456 | tf_op jit(solution)/shard_map/second/pallas_call | solution.py:183
  56.8 0.0 copy-start.4
  56.9 1.0 copy-done.4
  57.8 3.6 %first.1.bv_ref = f32[272,32,1024]{2,1,0:T(8,128)} custom-call(bf16[1024,1024]{1,0:T(8,128)(2,1)S(1)} %copy-done.1, bf16[1024,1024]{1,0:T(8,128)(2,1)S(1)} %copy-done.2, f32[8,1024]{1,0:T(8,128)S(1)} %copy-done.7, f32[6,8]{1,0:T(8,128)S(1)} %copy-done.8, f32[8,32,1024]{2,1,0:T(8,128)S(1)} %copy-done, f32[2,32,1024]{2,1,0:T(8,128)S(1)} %collective-permute-done.below_ref, ...), custom_call_target="tpu_custom_call" | custom-call | flops 1610612736 | bytes 7340032 | tf_op jit(solution)/shard_map/first/pallas_call | solution.py:237
  61.5 18.2 %all-to-all-done.1.w_ref = f32[32,32,256]{2,1,0:T(8,128)} async-done(((f32[32,32,256]{2,1,0:T(8,128)}), f32[32,32,256]{2,1,0:T(8,128)}, u32[]{:S(2)}, u32[]{:S(2)}) %all-to-all-start.1) | async-done | bytes 1048608 | tf_op jit(solution)/shard_map/all_to_all | solution.py:350
  79.6 5.6 %all-to-all-start.2 = ((f32[32,32,256]{2,1,0:T(8,128)}), f32[32,32,256]{2,1,0:T(8,128)}, u32[]{:S(2)}, u32[]{:S(2)}) async-start(f32[32,32,256]{2,1,0:T(8,128)} %bitcast.9), calls=%async_computation.2 | async-start | bytes 2097152 | tf_op jit(solution)/shard_map/all_to_all | solution.py:350
  85.3 1.8 %once.1 = (f32[8,32,1024]{2,1,0:T(8,128)S(1)}, f32[2,32,1024]{2,1,0:T(8,128)S(1)}, f32[2,32,1024]{2,1,0:T(8,128)S(1)}) custom-call(f32[272,32,1024]{2,1,0:T(8,128)} %first.1.bv_ref, f32[32,32,256]{2,1,0:T(8,128)} %all-to-all-done.1.w_ref), custom_call_target="tpu_custom_call" | custom-call | flops 1048576 | bytes 4194304 | tf_op jit(solution)/shard_map/once/pallas_call | solution.py:267
  87.1 1.3 %collective-permute-start.2 = (f32[2,32,1024]{2,1,0:T(8,128)S(1)}, f32[2,32,1024]{2,1,0:T(8,128)S(1)}, u32[]{:S(2)}, u32[]{:S(2)}) collective-permute-start(f32[2,32,1024]{2,1,0:T(8,128)S(1)} %get-tuple-element.27), channel_id=1, source_target_pairs={{0,32},{32,64},{64,96},{96,128},{128,160},{160,192},{192,224},{1,3... | collective-permute-start | bytes 786440 | tf_op jit(solution)/shard_map/ppermute | solution.py:355
  88.4 1.3 %collective-permute-start.3 = (f32[2,32,1024]{2,1,0:T(8,128)S(1)}, f32[2,32,1024]{2,1,0:T(8,128)S(1)}, u32[]{:S(2)}, u32[]{:S(2)}) collective-permute-start(f32[2,32,1024]{2,1,0:T(8,128)S(1)} %get-tuple-element.28), channel_id=1, source_target_pairs={{32,0},{64,32},{96,64},{128,96},{160,128},{192,160},{224,192},{33,... | collective-permute-start | bytes 786440 | tf_op jit(solution)/shard_map/ppermute | solution.py:356
  89.7 0.0 collective-permute-done.2.below_ref
  89.7 3.8 %collective-permute-done.3.above_ref = f32[2,32,1024]{2,1,0:T(8,128)S(1)} collective-permute-done((f32[2,32,1024]{2,1,0:T(8,128)S(1)}, f32[2,32,1024]{2,1,0:T(8,128)S(1)}, u32[]{:S(2)}, u32[]{:S(2)}) %collective-permute-start.3) | collective-permute-done | bytes 262176 | tf_op jit(solution)/shard_map/ppermute | solution.py:356
  93.6 4.9 %twice.1.both_ref = f32[34,8,32,1024]{3,2,1,0:T(8,128)} custom-call(bf16[1024,1024]{1,0:T(8,128)(2,1)S(1)} %copy-done.1, bf16[1024,1024]{1,0:T(8,128)(2,1)S(1)} %copy-done.3, f32[8,1024]{1,0:T(8,128)S(1)} %copy-done.7, f32[6,8]{1,0:T(8,128)S(1)} %copy-done.8, f32[8,32,1024]{2,1,0:T(8,128)S(1)} %copy-done, f32[272,32,1024]{2,1,0:T(8,128)} %first.1.bv_ref, ...), custom_call_target="tpu_custom_call" | custom-call | flops 1610612736 | bytes 9437184 | tf_op jit(solution)/shard_map/twice/pallas_call | solution.py:304
  98.4 13.4 %all-to-all-done.2.w_ref = f32[32,32,256]{2,1,0:T(8,128)} async-done(((f32[32,32,256]{2,1,0:T(8,128)}), f32[32,32,256]{2,1,0:T(8,128)}, u32[]{:S(2)}, u32[]{:S(2)}) %all-to-all-start.2) | async-done | bytes 1048608 | tf_op jit(solution)/shard_map/all_to_all | solution.py:350
  111.9 2.9 %finish.1 = (f32[8,32,1024]{2,1,0:T(8,128)}, f32[8,32,1024]{2,1,0:T(8,128)}) custom-call(f32[34,8,32,1024]{3,2,1,0:T(8,128)} %twice.1.both_ref, f32[32,32,256]{2,1,0:T(8,128)} %all-to-all-done.2.w_ref), custom_call_target="tpu_custom_call" | custom-call | flops 1048576 | bytes 5242880 | tf_op jit(solution)/shard_map/finish/pallas_call | solution.py:331
  (17 shorter events, 0.0 us)
Async XLA Ops:
  2.7 39.8 %all-to-all-start = ((f32[32,32,256]{2,1,0:T(8,128)}), f32[32,32,256]{2,1,0:T(8,128)S(1)}, u32[]{:S(2)}, u32[]{:S(2)}) async-start(f32[32,32,256]{2,1,0:T(8,128)} %bitcast.11), calls=%async_computation | async-start | bytes 2097152 | tf_op jit(solution)/shard_map/all_to_all | solution.py:350
  15.5 12.2 %collective-permute-start = (f32[2,32,1024]{2,1,0:T(8,128)S(1)}, f32[2,32,1024]{2,1,0:T(8,128)S(1)}, u32[]{:S(2)}, u32[]{:S(2)}) collective-permute-start(f32[2,32,1024]{2,1,0:T(8,128)S(1)} %get-tuple-element.31), channel_id=1, source_target_pairs={{0,32},{32,64},{64,96},{96,128},{128,160},{160,192},{192,224},{1,3... | collective-permute-start | bytes 786440 | tf_op jit(solution)/shard_map/ppermute | solution.py:355
  16.8 10.9 %collective-permute-start.1 = (f32[2,32,1024]{2,1,0:T(8,128)S(1)}, f32[2,32,1024]{2,1,0:T(8,128)S(1)}, u32[]{:S(2)}, u32[]{:S(2)}) collective-permute-start(f32[2,32,1024]{2,1,0:T(8,128)S(1)} %get-tuple-element.30), channel_id=1, source_target_pairs={{32,0},{64,32},{96,64},{128,96},{160,128},{192,160},{224,192},{33,... | collective-permute-start | bytes 786440 | tf_op jit(solution)/shard_map/ppermute | solution.py:356
  27.7 19.3 %copy-start.5 = (f32[2,32,1024]{2,1,0:T(8,128)}, f32[2,32,1024]{2,1,0:T(8,128)S(1)}, u32[]{:S(2)}) copy-start(f32[2,32,1024]{2,1,0:T(8,128)S(1)} %collective-permute-done.1.above_ref) | copy-start | bytes 786436
  47.0 32.7 %all-to-all-start.1 = ((f32[32,32,256]{2,1,0:T(8,128)}), f32[32,32,256]{2,1,0:T(8,128)}, u32[]{:S(2)}, u32[]{:S(2)}) async-start(f32[32,32,256]{2,1,0:T(8,128)} %bitcast.6), calls=%async_computation.1 | async-start | bytes 2097152 | tf_op jit(solution)/shard_map/all_to_all | solution.py:350
  52.6 5.2 %copy-start = (f32[8,32,1024]{2,1,0:T(8,128)S(1)}, f32[8,32,1024]{2,1,0:T(8,128)}, u32[]{:S(2)}) copy-start(f32[8,32,1024]{2,1,0:T(8,128)} %v_ref.5) | copy-start | bytes 3145732
  52.6 5.2 %copy-start.1 = (bf16[1024,1024]{1,0:T(8,128)(2,1)S(1)}, bf16[1024,1024]{1,0:T(8,128)(2,1)}, u32[]{:S(2)}) copy-start(bf16[1024,1024]{1,0:T(8,128)(2,1)} %get-tuple-element.16.high_ref) | copy-start | bytes 6291460
  52.6 5.2 %copy-start.2 = (bf16[1024,1024]{1,0:T(8,128)(2,1)S(1)}, bf16[1024,1024]{1,0:T(8,128)(2,1)}, u32[]{:S(2)}) copy-start(bf16[1024,1024]{1,0:T(8,128)(2,1)} %get-tuple-element.17.low_ref) | copy-start | bytes 6291460
  52.6 5.2 %copy-start.6 = (f32[2,32,1024]{2,1,0:T(8,128)S(1)}, f32[2,32,1024]{2,1,0:T(8,128)}, u32[]{:S(2)}) copy-start(f32[2,32,1024]{2,1,0:T(8,128)} %copy-done.5) | copy-start | bytes 786436
  52.6 5.2 %copy-start.7 = (f32[8,1024]{1,0:T(8,128)S(1)}, f32[8,1024]{1,0:T(8,128)}, u32[]{:S(2)}) copy-start(f32[8,1024]{1,0:T(8,128)} %get-tuple-element.18.exits_ref) | copy-start | bytes 98308
  52.6 5.2 %copy-start.8 = (f32[6,8]{1,0:T(8,128)S(1)}, f32[6,8]{1,0:T(8,128)}, u32[]{:S(2)}) copy-start(f32[6,8]{1,0:T(8,128)} %get-tuple-element.19.coef_ref) | copy-start | bytes 580
  56.8 1.0 copy-start.4
  79.6 32.2 %all-to-all-start.2 = ((f32[32,32,256]{2,1,0:T(8,128)}), f32[32,32,256]{2,1,0:T(8,128)}, u32[]{:S(2)}, u32[]{:S(2)}) async-start(f32[32,32,256]{2,1,0:T(8,128)} %bitcast.9), calls=%async_computation.2 | async-start | bytes 2097152 | tf_op jit(solution)/shard_map/all_to_all | solution.py:350
  85.3 8.3 %copy-start.3 = (bf16[1024,1024]{1,0:T(8,128)(2,1)S(1)}, bf16[1024,1024]{1,0:T(8,128)(2,1)}, u32[]{:S(2)}) copy-start(bf16[1024,1024]{1,0:T(8,128)(2,1)} %get-tuple-element.17.low_ref) | copy-start | bytes 6291460
  87.1 2.6 %collective-permute-start.2 = (f32[2,32,1024]{2,1,0:T(8,128)S(1)}, f32[2,32,1024]{2,1,0:T(8,128)S(1)}, u32[]{:S(2)}, u32[]{:S(2)}) collective-permute-start(f32[2,32,1024]{2,1,0:T(8,128)S(1)} %get-tuple-element.27), channel_id=1, source_target_pairs={{0,32},{32,64},{64,96},{96,128},{128,160},{160,192},{192,224},{1,3... | collective-permute-start | bytes 786440 | tf_op jit(solution)/shard_map/ppermute | solution.py:355
  88.4 5.1 %collective-permute-start.3 = (f32[2,32,1024]{2,1,0:T(8,128)S(1)}, f32[2,32,1024]{2,1,0:T(8,128)S(1)}, u32[]{:S(2)}, u32[]{:S(2)}) collective-permute-start(f32[2,32,1024]{2,1,0:T(8,128)S(1)} %get-tuple-element.28), channel_id=1, source_target_pairs={{32,0},{64,32},{96,64},{128,96},{160,128},{192,160},{224,192},{33,... | collective-permute-start | bytes 786440 | tf_op jit(solution)/shard_map/ppermute | solution.py:356

commit v4 on v3

--- a/solution.py
+++ b/solution.py
@@ -165,15 +165,15 @@
     )(v)
 
 
-def turned_kernel(both_ref, exits_ref, mass_ref, out_ref, up, down):
+def turned_kernel(high_ref, low_ref, exits_ref, mass_ref, out_ref, up, down):
     @pl.when(pl.program_id(0) == 0)
     def _():
         up[...], down[...] = halves(mass_ref[...])
 
     tall = out_ref.shape[0]
     rows = pl.ds(pl.multiple_of(pl.program_id(0) * tall, tall), tall)
-    left = both_ref[0]
-    total = mm(left, up[...]) + mm(left, down[...]) + mm(both_ref[1], up[...])
+    left = high_ref[0]
+    total = mm(left, up[...]) + mm(left, down[...]) + mm(low_ref[0], up[...])
     turn = exits_ref[...].T
     out_ref[...] = (total - mass_ref[rows, :] * turn[:, 0:1]) * turn[:, 4:5]
 
@@ -184,7 +184,8 @@
         turned_kernel,
         grid=(order // tall,),
         in_specs=[
-            pl.BlockSpec((2, tall, order), lambda i: (0, i, 0)),
+            pl.BlockSpec((1, tall, order), lambda i: (0, i, 0)),
+            pl.BlockSpec((1, tall, order), lambda i: (1, i, 0)),
             pl.BlockSpec((8, tall), lambda i: (0, i)),
             WHOLE,
         ],
@@ -194,7 +195,7 @@
         compiler_params=params(32),
         cost_estimate=pl.CostEstimate(flops=3 << 29, bytes_accessed=6 << 20, transcendentals=0),
         name="second",
-    )(both, exits, mass)
+    )(both, both, exits, mass)
 
 
 def product(x, high_ref, low_ref, cols):
@@ -313,15 +314,15 @@
     )(high, low, exits, coef, v, bv, s, below, above)
 
 
-def finish_kernel(both_ref, w_ref, out_t_ref, out_s_ref):
+def finish_kernel(step_ref, trans_ref, w_ref, out_t_ref, out_s_ref):
     levels, _, order = out_s_ref.shape
     parts = order // LANES
     for m in range(levels):
         for p in range(parts):
             cols = pl.ds(p * LANES, LANES)
             more = w_ref[m * parts + p]
-            out_s_ref[m, :, cols] = both_ref[0, m, :, cols] + more
-            out_t_ref[m, :, cols] = both_ref[1, m, :, cols] + 0.2 * more
+            out_s_ref[m, :, cols] = step_ref[0, m, :, cols] + more
+            out_t_ref[m, :, cols] = trans_ref[0, m, :, cols] + 0.2 * more
 
 
 def finish(both, w, tall=4):
@@ -332,7 +333,8 @@
         finish_kernel,
         grid=(levels // tall,),
         in_specs=[
-            pl.BlockSpec((2, tall, rows, order), lambda i: (0, i, 0, 0)),
+            pl.BlockSpec((1, tall, rows, order), lambda i: (0, i, 0, 0)),
+            pl.BlockSpec((1, tall, rows, order), lambda i: (1, i, 0, 0)),
             pl.BlockSpec((tall * (order // LANES), rows, LANES), lambda i: (i, 0, 0)),
         ],
         out_specs=[block, block],
@@ -340,7 +342,7 @@
         compiler_params=params(32),
         cost_estimate=pl.CostEstimate(flops=1 << 20, bytes_accessed=5 << 20, transcendentals=0),
         name="finish",
-    )(both, w)
+    )(both, both, w)
 
 
 def swap(chunks):

time: 115 us -> 115 us (level)
  no operation moved by 1% of the time
where the time goes in v4:
time: 115 us
  waiting for transfers between devices  49.9 us (43%)
  Pallas kernels  33.8 us (29%)
  starting transfers between devices  28.1 us (24%)
  local copies, waits for them, and re-layouts  2.07 us (2%)
    all_to_all x3, waiting for transfers between devices, swap(): lax.all_to_all(chunks, 'comp', split_axis=0, concat_axis=0, axis_index_gr...  46.1 us
    all_to_all x3, starting transfers between devices, swap(): lax.all_to_all(chunks, 'comp', split_axis=0, concat_axis=0, axis_index_gr...  22.9 us
    pallas_call x1, Pallas kernels, prepare(): pl.pallas_call(prepare_kernel, grid=(order // tall,), in_specs=[SCALARS,...  9.58 us
    pallas_call x2, Pallas kernels, turned(): pl.pallas_call(turned_kernel, grid=(order // tall,), in_specs=[pl.BlockSp...  8.95 us
    pallas_call x1, Pallas kernels, twice(): pl.pallas_call(twice_kernel, grid=(1,), in_specs=[WHOLE, WHOLE, WHOLE, SC...  4.89 us
    ppermute x2, waiting for transfers between devices, neighbours(): above = lax.ppermute(low, 'ctr', [(i + 1, i) for i in range(count - 1)])  3.83 us
    pallas_call x1, Pallas kernels, first(): pl.pallas_call(first_kernel, grid=(1,), in_specs=[WHOLE, WHOLE, WHOLE, SC...  3.61 us
    pallas_call x1, Pallas kernels, finish(): pl.pallas_call(finish_kernel, grid=(levels // tall,), in_specs=[pl.BlockS...  2.89 us
  transfers between devices with their start and end apart: 7, of which 4 were waited for; matrix products, arithmetic and copies ran while one was open for 1% of the time, Pallas kernels for 21%

profile of v4, /device:TPU:8, one launch (start us, length us, event | category | flops | bytes accessed | tf_op | source)
XLA Modules:
  0.0 114.7 jit_solution(11686260760253575446)
XLA Ops:
  0.6 2.1 %pack.1 = f32[8,4,32,256]{3,2,1,0:T(8,128)} custom-call(f32[8,32,1024]{2,1,0:T(8,128)} %v_ref.5), custom_call_target="tpu_custom_call" | custom-call | bytes 2097152 | tf_op jit(solution)/shard_map/pack/pallas_call | solution.py:156
  2.7 11.7 %all-to-all-start = ((f32[32,32,256]{2,1,0:T(8,128)}), f32[32,32,256]{2,1,0:T(8,128)S(1)}, u32[]{:S(2)}, u32[]{:S(2)}) async-start(f32[32,32,256]{2,1,0:T(8,128)} %bitcast.11), calls=%async_computation | async-start | bytes 2097152 | tf_op jit(solution)/shard_map/all_to_all | solution.py:352
  14.4 1.1 fusion
  15.5 1.3 %collective-permute-start = (f32[2,32,1024]{2,1,0:T(8,128)S(1)}, f32[2,32,1024]{2,1,0:T(8,128)S(1)}, u32[]{:S(2)}, u32[]{:S(2)}) collective-permute-start(f32[2,32,1024]{2,1,0:T(8,128)S(1)} %get-tuple-element.31), channel_id=1, source_target_pairs={{0,32},{32,64},{64,96},{96,128},{128,160},{160,192},{192,224},{1,3... | collective-permute-start | bytes 786440 | tf_op jit(solution)/shard_map/ppermute | solution.py:357
  16.8 1.3 %collective-permute-start.1 = (f32[2,32,1024]{2,1,0:T(8,128)S(1)}, f32[2,32,1024]{2,1,0:T(8,128)S(1)}, u32[]{:S(2)}, u32[]{:S(2)}) collective-permute-start(f32[2,32,1024]{2,1,0:T(8,128)S(1)} %get-tuple-element.30), channel_id=1, source_target_pairs={{32,0},{64,32},{96,64},{128,96},{160,128},{192,160},{224,192},{33,... | collective-permute-start | bytes 786440 | tf_op jit(solution)/shard_map/ppermute | solution.py:358
  18.1 9.6 %prepare.1 = (bf16[1024,1024]{1,0:T(8,128)(2,1)}, bf16[1024,1024]{1,0:T(8,128)(2,1)}, f32[8,1024]{1,0:T(8,128)}, bf16[17,1024,1024]{2,1,0:T(8,128)(2,1)}, f32[8704,1024]{1,0:T(8,128)}, /*index=5*/f32[6,8]{1,0:T(8,128)}) custom-call(f32[64]{0:T(128)} %rate_ref.1, s32[64]{0:T(128)} %code_ref.1, s32[1]{0:T(128)} %bitcast.start_ref, f32[1,64]{1,0:T(1,128)} %bitcast.12, ...), custom_call_target="tpu_custom_call" | custom-call | flops 134217728 | bytes 16777216 | tf_op jit(solution)/shard_map/prepare/pallas_call | solution.py:125
  27.7 0.0 collective-permute-done.below_ref
  27.7 14.8 %all-to-all-done = f32[32,32,256]{2,1,0:T(8,128)S(1)} async-done(((f32[32,32,256]{2,1,0:T(8,128)}), f32[32,32,256]{2,1,0:T(8,128)S(1)}, u32[]{:S(2)}, u32[]{:S(2)}) %all-to-all-start) | async-done | bytes 1048608 | tf_op jit(solution)/shard_map/all_to_all | solution.py:352
  42.5 4.5 %second.2.mass_ref = f32[1024,256]{1,0:T(8,128)} custom-call(bf16[17,1024,1024]{2,1,0:T(8,128)(2,1)} %get-tuple-element.20.high_ref.low_ref, bf16[17,1024,1024]{2,1,0:T(8,128)(2,1)} %get-tuple-element.20.high_ref.low_ref, f32[8704,1024]{1,0:T(8,128)} %get-tuple-element.21.exits_ref, f32[1024,256]{1,0:T(8,128)S(1)} %bitcast.8), custom_call_target="tpu_custom_call" | custom-call | flops 1610612736 | bytes 6291456 | tf_op jit(solution)/shard_map/second/pallas_call | solution.py:183
  46.9 5.6 %all-to-all-start.1 = ((f32[32,32,256]{2,1,0:T(8,128)}), f32[32,32,256]{2,1,0:T(8,128)}, u32[]{:S(2)}, u32[]{:S(2)}) async-start(f32[32,32,256]{2,1,0:T(8,128)} %bitcast.6), calls=%async_computation.1 | async-start | bytes 2097152 | tf_op jit(solution)/shard_map/all_to_all | solution.py:352
  52.5 0.0 copy-start
  52.6 4.5 %second.3 = f32[1024,256]{1,0:T(8,128)S(1)} custom-call(bf16[17,1024,1024]{2,1,0:T(8,128)(2,1)} %get-tuple-element.20.high_ref.low_ref, bf16[17,1024,1024]{2,1,0:T(8,128)(2,1)} %get-tuple-element.20.high_ref.low_ref, f32[8704,1024]{1,0:T(8,128)} %get-tuple-element.21.exits_ref, f32[1024,256]{1,0:T(8,128)} %second.2.mass_ref), custom_call_target="tpu_custom_call" | custom-call | flops 1610612736 | bytes 6291456 | tf_op jit(solution)/shard_map/second/pallas_call | solution.py:183
  57.1 0.0 copy-start.4
  57.1 1.0 copy-done.4
  58.1 3.6 %first.1.bv_ref = f32[272,32,1024]{2,1,0:T(8,128)} custom-call(bf16[1024,1024]{1,0:T(8,128)(2,1)S(1)} %copy-done.1, bf16[1024,1024]{1,0:T(8,128)(2,1)S(1)} %copy-done.2, f32[8,1024]{1,0:T(8,128)S(1)} %copy-done.7, f32[6,8]{1,0:T(8,128)S(1)} %copy-done.8, f32[8,32,1024]{2,1,0:T(8,128)S(1)} %copy-done, f32[2,32,1024]{2,1,0:T(8,128)S(1)} %collective-permute-done.below_ref, ...), custom_call_target="tpu_custom_call" | custom-call | flops 1610612736 | bytes 7340032 | tf_op jit(solution)/shard_map/first/pallas_call | solution.py:238
  61.7 17.9 %all-to-all-done.1.w_ref = f32[32,32,256]{2,1,0:T(8,128)} async-done(((f32[32,32,256]{2,1,0:T(8,128)}), f32[32,32,256]{2,1,0:T(8,128)}, u32[]{:S(2)}, u32[]{:S(2)}) %all-to-all-start.1) | async-done | bytes 1048608 | tf_op jit(solution)/shard_map/all_to_all | solution.py:352
  79.6 5.6 %all-to-all-start.2 = ((f32[32,32,256]{2,1,0:T(8,128)}), f32[32,32,256]{2,1,0:T(8,128)}, u32[]{:S(2)}, u32[]{:S(2)}) async-start(f32[32,32,256]{2,1,0:T(8,128)} %bitcast.9), calls=%async_computation.2 | async-start | bytes 2097152 | tf_op jit(solution)/shard_map/all_to_all | solution.py:352
  85.2 1.8 %once.1 = (f32[8,32,1024]{2,1,0:T(8,128)S(1)}, f32[2,32,1024]{2,1,0:T(8,128)S(1)}, f32[2,32,1024]{2,1,0:T(8,128)S(1)}) custom-call(f32[272,32,1024]{2,1,0:T(8,128)} %first.1.bv_ref, f32[32,32,256]{2,1,0:T(8,128)} %all-to-all-done.1.w_ref), custom_call_target="tpu_custom_call" | custom-call | flops 1048576 | bytes 4194304 | tf_op jit(solution)/shard_map/once/pallas_call | solution.py:268
  87.1 1.3 %collective-permute-start.2 = (f32[2,32,1024]{2,1,0:T(8,128)S(1)}, f32[2,32,1024]{2,1,0:T(8,128)S(1)}, u32[]{:S(2)}, u32[]{:S(2)}) collective-permute-start(f32[2,32,1024]{2,1,0:T(8,128)S(1)} %get-tuple-element.27), channel_id=1, source_target_pairs={{0,32},{32,64},{64,96},{96,128},{128,160},{160,192},{192,224},{1,3... | collective-permute-start | bytes 786440 | tf_op jit(solution)/shard_map/ppermute | solution.py:357
  88.4 1.3 %collective-permute-start.3 = (f32[2,32,1024]{2,1,0:T(8,128)S(1)}, f32[2,32,1024]{2,1,0:T(8,128)S(1)}, u32[]{:S(2)}, u32[]{:S(2)}) collective-permute-start(f32[2,32,1024]{2,1,0:T(8,128)S(1)} %get-tuple-element.28), channel_id=1, source_target_pairs={{32,0},{64,32},{96,64},{128,96},{160,128},{192,160},{224,192},{33,... | collective-permute-start | bytes 786440 | tf_op jit(solution)/shard_map/ppermute | solution.py:358
  89.7 3.8 %collective-permute-done.3.above_ref = f32[2,32,1024]{2,1,0:T(8,128)S(1)} collective-permute-done((f32[2,32,1024]{2,1,0:T(8,128)S(1)}, f32[2,32,1024]{2,1,0:T(8,128)S(1)}, u32[]{:S(2)}, u32[]{:S(2)}) %collective-permute-start.3) | collective-permute-done | bytes 262176 | tf_op jit(solution)/shard_map/ppermute | solution.py:358
  93.5 4.9 %twice.1.step_ref.trans_ref = f32[34,8,32,1024]{3,2,1,0:T(8,128)} custom-call(bf16[1024,1024]{1,0:T(8,128)(2,1)S(1)} %copy-done.1, bf16[1024,1024]{1,0:T(8,128)(2,1)S(1)} %copy-done.3, f32[8,1024]{1,0:T(8,128)S(1)} %copy-done.7, f32[6,8]{1,0:T(8,128)S(1)} %copy-done.8, f32[8,32,1024]{2,1,0:T(8,128)S(1)} %copy-done, f32[272,32,1024]{2,1,0:T(8,128)} %first.1.bv_ref, ...), custom_call_target="tpu_custom_call" | custom-call | flops 1610612736 | bytes 9437184 | tf_op jit(solution)/shard_map/twice/pallas_call | solution.py:305
  98.4 13.4 %all-to-all-done.2.w_ref = f32[32,32,256]{2,1,0:T(8,128)} async-done(((f32[32,32,256]{2,1,0:T(8,128)}), f32[32,32,256]{2,1,0:T(8,128)}, u32[]{:S(2)}, u32[]{:S(2)}) %all-to-all-start.2) | async-done | bytes 1048608 | tf_op jit(solution)/shard_map/all_to_all | solution.py:352
  111.8 2.9 %finish.1 = (f32[8,32,1024]{2,1,0:T(8,128)}, f32[8,32,1024]{2,1,0:T(8,128)}) custom-call(f32[34,8,32,1024]{3,2,1,0:T(8,128)} %twice.1.step_ref.trans_ref, f32[34,8,32,1024]{3,2,1,0:T(8,128)} %twice.1.step_ref.trans_ref, f32[32,32,256]{2,1,0:T(8,128)} %all-to-all-done.2.w_ref), custom_call_target="tpu_custom_call" | custom-call | flops 1048576 | bytes 5242880 | tf_op jit(solution)/shard_map/finish/pallas_call | solution.py:332
  (17 shorter events, 0.0 us)
Async XLA Ops:
  2.7 39.8 %all-to-all-start = ((f32[32,32,256]{2,1,0:T(8,128)}), f32[32,32,256]{2,1,0:T(8,128)S(1)}, u32[]{:S(2)}, u32[]{:S(2)}) async-start(f32[32,32,256]{2,1,0:T(8,128)} %bitcast.11), calls=%async_computation | async-start | bytes 2097152 | tf_op jit(solution)/shard_map/all_to_all | solution.py:352
  15.5 12.2 %collective-permute-start = (f32[2,32,1024]{2,1,0:T(8,128)S(1)}, f32[2,32,1024]{2,1,0:T(8,128)S(1)}, u32[]{:S(2)}, u32[]{:S(2)}) collective-permute-start(f32[2,32,1024]{2,1,0:T(8,128)S(1)} %get-tuple-element.31), channel_id=1, source_target_pairs={{0,32},{32,64},{64,96},{96,128},{128,160},{160,192},{192,224},{1,3... | collective-permute-start | bytes 786440 | tf_op jit(solution)/shard_map/ppermute | solution.py:357
  16.8 10.9 %collective-permute-start.1 = (f32[2,32,1024]{2,1,0:T(8,128)S(1)}, f32[2,32,1024]{2,1,0:T(8,128)S(1)}, u32[]{:S(2)}, u32[]{:S(2)}) collective-permute-start(f32[2,32,1024]{2,1,0:T(8,128)S(1)} %get-tuple-element.30), channel_id=1, source_target_pairs={{32,0},{64,32},{96,64},{128,96},{160,128},{192,160},{224,192},{33,... | collective-permute-start | bytes 786440 | tf_op jit(solution)/shard_map/ppermute | solution.py:358
  27.7 19.2 %copy-start.5 = (f32[2,32,1024]{2,1,0:T(8,128)}, f32[2,32,1024]{2,1,0:T(8,128)S(1)}, u32[]{:S(2)}) copy-start(f32[2,32,1024]{2,1,0:T(8,128)S(1)} %collective-permute-done.1.above_ref) | copy-start | bytes 786436
  46.9 32.7 %all-to-all-start.1 = ((f32[32,32,256]{2,1,0:T(8,128)}), f32[32,32,256]{2,1,0:T(8,128)}, u32[]{:S(2)}, u32[]{:S(2)}) async-start(f32[32,32,256]{2,1,0:T(8,128)} %bitcast.6), calls=%async_computation.1 | async-start | bytes 2097152 | tf_op jit(solution)/shard_map/all_to_all | solution.py:352
  52.5 5.5 %copy-start = (f32[8,32,1024]{2,1,0:T(8,128)S(1)}, f32[8,32,1024]{2,1,0:T(8,128)}, u32[]{:S(2)}) copy-start(f32[8,32,1024]{2,1,0:T(8,128)} %v_ref.5) | copy-start | bytes 3145732
  52.6 5.5 %copy-start.1 = (bf16[1024,1024]{1,0:T(8,128)(2,1)S(1)}, bf16[1024,1024]{1,0:T(8,128)(2,1)}, u32[]{:S(2)}) copy-start(bf16[1024,1024]{1,0:T(8,128)(2,1)} %get-tuple-element.16.high_ref) | copy-start | bytes 6291460
  52.6 5.5 %copy-start.2 = (bf16[1024,1024]{1,0:T(8,128)(2,1)S(1)}, bf16[1024,1024]{1,0:T(8,128)(2,1)}, u32[]{:S(2)}) copy-start(bf16[1024,1024]{1,0:T(8,128)(2,1)} %get-tuple-element.17.low_ref) | copy-start | bytes 6291460
  52.6 5.5 %copy-start.6 = (f32[2,32,1024]{2,1,0:T(8,128)S(1)}, f32[2,32,1024]{2,1,0:T(8,128)}, u32[]{:S(2)}) copy-start(f32[2,32,1024]{2,1,0:T(8,128)} %copy-done.5) | copy-start | bytes 786436
  52.6 5.5 %copy-start.7 = (f32[8,1024]{1,0:T(8,128)S(1)}, f32[8,1024]{1,0:T(8,128)}, u32[]{:S(2)}) copy-start(f32[8,1024]{1,0:T(8,128)} %get-tuple-element.18.exits_ref) | copy-start | bytes 98308
  52.6 5.5 %copy-start.8 = (f32[6,8]{1,0:T(8,128)S(1)}, f32[6,8]{1,0:T(8,128)}, u32[]{:S(2)}) copy-start(f32[6,8]{1,0:T(8,128)} %get-tuple-element.19.coef_ref) | copy-start | bytes 580
  57.1 1.0 copy-start.4
  79.6 32.2 %all-to-all-start.2 = ((f32[32,32,256]{2,1,0:T(8,128)}), f32[32,32,256]{2,1,0:T(8,128)}, u32[]{:S(2)}, u32[]{:S(2)}) async-start(f32[32,32,256]{2,1,0:T(8,128)} %bitcast.9), calls=%async_computation.2 | async-start | bytes 2097152 | tf_op jit(solution)/shard_map/all_to_all | solution.py:352
  85.2 8.3 %copy-start.3 = (bf16[1024,1024]{1,0:T(8,128)(2,1)S(1)}, bf16[1024,1024]{1,0:T(8,128)(2,1)}, u32[]{:S(2)}) copy-start(bf16[1024,1024]{1,0:T(8,128)(2,1)} %get-tuple-element.17.low_ref) | copy-start | bytes 6291460
  87.1 2.6 %collective-permute-start.2 = (f32[2,32,1024]{2,1,0:T(8,128)S(1)}, f32[2,32,1024]{2,1,0:T(8,128)S(1)}, u32[]{:S(2)}, u32[]{:S(2)}) collective-permute-start(f32[2,32,1024]{2,1,0:T(8,128)S(1)} %get-tuple-element.27), channel_id=1, source_target_pairs={{0,32},{32,64},{64,96},{96,128},{128,160},{160,192},{192,224},{1,3... | collective-permute-start | bytes 786440 | tf_op jit(solution)/shard_map/ppermute | solution.py:357
  88.4 5.1 %collective-permute-start.3 = (f32[2,32,1024]{2,1,0:T(8,128)S(1)}, f32[2,32,1024]{2,1,0:T(8,128)S(1)}, u32[]{:S(2)}, u32[]{:S(2)}) collective-permute-start(f32[2,32,1024]{2,1,0:T(8,128)S(1)} %get-tuple-element.28), channel_id=1, source_target_pairs={{32,0},{64,32},{96,64},{128,96},{160,128},{192,160},{224,192},{33,... | collective-permute-start | bytes 786440 | tf_op jit(solution)/shard_map/ppermute | solution.py:358

commit v5 on v3

--- a/solution.py
+++ b/solution.py
@@ -368,7 +368,6 @@
         level_rate, level_code, start, rates_first, blocks_first, rates_second, blocks_second, levels, count
     )
 
-    turned_mass, below, above = lax.optimization_barrier((turned_mass, below, above))
     w_one = turned(sec_both, sec_exits, turned_mass)
     back_one = swap(w_one.reshape(count, rows, LANES))
     bv = first(fst_high, fst_low, exits, coef, initial, below, above)

time: 115 us -> 119 us (1.035)
  local copies, waits for them, and re-layouts: 2.07 us -> 4.8 us
    ppermute x2, waiting for transfers between devices: 3.83 us -> 7.66 us  [neighbours(): above = lax.ppermute(low, 'ctr', [(i + 1, i) for i in range(count - 1)])]
    unnamed x18, local copies, waits for them, and re-layouts: 1 us -> 4.76 us
    all_to_all x3, waiting for transfers between devices: 46.4 us -> 43.1 us  [swap(): lax.all_to_all(chunks, 'comp', split_axis=0, concat_axis=0, axis_index_gr...]
  transfers between devices with their start and end apart: 7 -> 7, of which waited for: 4 -> 5; matrix products, arithmetic and copies ran while one was open for 1% -> 0% of each run, Pallas kernels for 21% -> 20%
where the time goes in v5:
time: 119 us; the launch traced here: 118 us
  waiting for transfers between devices  50.7 us (43%)
  Pallas kernels  33.4 us (28%)
  starting transfers between devices  28.1 us (24%)
  local copies, waits for them, and re-layouts  4.8 us (4%)
    all_to_all x3, waiting for transfers between devices, swap(): lax.all_to_all(chunks, 'comp', split_axis=0, concat_axis=0, axis_index_gr...  43.1 us
    all_to_all x3, starting transfers between devices, swap(): lax.all_to_all(chunks, 'comp', split_axis=0, concat_axis=0, axis_index_gr...  22.9 us
    pallas_call x1, Pallas kernels, prepare(): pl.pallas_call(prepare_kernel, grid=(order // tall,), in_specs=[SCALARS,...  9.54 us
    pallas_call x2, Pallas kernels, turned(): pl.pallas_call(turned_kernel, grid=(order // tall,), in_specs=[pl.BlockSp...  8.69 us
    ppermute x2, waiting for transfers between devices, neighbours(): above = lax.ppermute(low, 'ctr', [(i + 1, i) for i in range(count - 1)])  7.66 us
    pallas_call x1, Pallas kernels, twice(): pl.pallas_call(twice_kernel, grid=(1,), in_specs=[WHOLE, WHOLE, WHOLE, SC...  4.83 us
    unnamed x18, local copies, waits for them, and re-layouts  4.76 us
    pallas_call x1, Pallas kernels, first(): pl.pallas_call(first_kernel, grid=(1,), in_specs=[WHOLE, WHOLE, WHOLE, SC...  3.6 us
  transfers between devices with their start and end apart: 7, of which 5 were waited for; matrix products, arithmetic and copies ran while one was open for 0% of the time, Pallas kernels for 20%

profile of v5, /device:TPU:8, one launch (start us, length us, event | category | flops | bytes accessed | tf_op | source)
XLA Modules:
  0.0 117.9 jit_solution(982855583437322167)
XLA Ops:
  0.6 2.1 %pack.1 = f32[8,4,32,256]{3,2,1,0:T(8,128)} custom-call(f32[8,32,1024]{2,1,0:T(8,128)} %v_ref.5), custom_call_target="tpu_custom_call" | custom-call | bytes 2097152 | tf_op jit(solution)/shard_map/pack/pallas_call | solution.py:156
  2.7 11.7 %all-to-all-start = ((f32[32,32,256]{2,1,0:T(8,128)}), f32[32,32,256]{2,1,0:T(8,128)S(1)}, u32[]{:S(2)}, u32[]{:S(2)}) async-start(f32[32,32,256]{2,1,0:T(8,128)} %bitcast.11), calls=%async_computation | async-start | bytes 2097152 | tf_op jit(solution)/shard_map/all_to_all | solution.py:350
  14.4 9.5 %prepare.1 = (bf16[1024,1024]{1,0:T(8,128)(2,1)}, bf16[1024,1024]{1,0:T(8,128)(2,1)}, f32[8,1024]{1,0:T(8,128)}, bf16[17,1024,1024]{2,1,0:T(8,128)(2,1)}, f32[8704,1024]{1,0:T(8,128)}, /*index=5*/f32[6,8]{1,0:T(8,128)}) custom-call(f32[64]{0:T(128)} %rate_ref.1, s32[64]{0:T(128)} %code_ref.1, s32[1]{0:T(128)} %bitcast.start_ref, f32[1,64]{1,0:T(1,128)} %bitcast.12, ...), custom_call_target="tpu_custom_call" | custom-call | flops 134217728 | bytes 16777216 | tf_op jit(solution)/shard_map/prepare/pallas_call | solution.py:125
  23.9 18.5 %all-to-all-done = f32[32,32,256]{2,1,0:T(8,128)S(1)} async-done(((f32[32,32,256]{2,1,0:T(8,128)}), f32[32,32,256]{2,1,0:T(8,128)S(1)}, u32[]{:S(2)}, u32[]{:S(2)}) %all-to-all-start) | async-done | bytes 1048608 | tf_op jit(solution)/shard_map/all_to_all | solution.py:350
  42.5 1.0 copy-done.5
  43.4 1.2 %copy-done.6 = f32[32,32,256]{2,1,0:T(8,128)S(1)} copy-done((f32[32,32,256]{2,1,0:T(8,128)S(1)}, f32[32,32,256]{2,1,0:T(8,128)}, u32[]{:S(2)}) %copy-start.6) | copy-done | bytes 1048600
  44.7 4.7 %second.2.mass_ref = f32[1024,256]{1,0:T(8,128)} custom-call(bf16[17,1024,1024]{2,1,0:T(8,128)(2,1)} %get-tuple-element.17.both_ref, f32[8704,1024]{1,0:T(8,128)} %get-tuple-element.18.exits_ref, f32[1024,256]{1,0:T(8,128)S(1)} %bitcast.9), custom_call_target="tpu_custom_call" | custom-call | flops 1610612736 | bytes 6291456 | tf_op jit(solution)/shard_map/second/pallas_call | solution.py:183
  49.3 5.6 %all-to-all-start.1 = ((f32[32,32,256]{2,1,0:T(8,128)}), f32[32,32,256]{2,1,0:T(8,128)}, u32[]{:S(2)}, u32[]{:S(2)}) async-start(f32[32,32,256]{2,1,0:T(8,128)} %bitcast.6), calls=%async_computation.1 | async-start | bytes 2097152 | tf_op jit(solution)/shard_map/all_to_all | solution.py:350
  55.0 1.3 %collective-permute-start = (f32[2,32,1024]{2,1,0:T(8,128)S(1)}, f32[2,32,1024]{2,1,0:T(8,128)S(1)}, u32[]{:S(2)}, u32[]{:S(2)}) collective-permute-start(f32[2,32,1024]{2,1,0:T(8,128)S(1)} %get-tuple-element.25), channel_id=1, source_target_pairs={{0,32},{32,64},{64,96},{96,128},{128,160},{160,192},{192,224},{1,3... | collective-permute-start | bytes 786440 | tf_op jit(solution)/shard_map/ppermute | solution.py:355
  56.3 1.3 %collective-permute-start.1 = (f32[2,32,1024]{2,1,0:T(8,128)S(1)}, f32[2,32,1024]{2,1,0:T(8,128)S(1)}, u32[]{:S(2)}, u32[]{:S(2)}) collective-permute-start(f32[2,32,1024]{2,1,0:T(8,128)S(1)} %get-tuple-element.24), channel_id=1, source_target_pairs={{32,0},{64,32},{96,64},{128,96},{160,128},{192,160},{224,192},{33,... | collective-permute-start | bytes 786440 | tf_op jit(solution)/shard_map/ppermute | solution.py:356
  57.6 3.8 %collective-permute-done.1.above_ref = f32[2,32,1024]{2,1,0:T(8,128)S(1)} collective-permute-done((f32[2,32,1024]{2,1,0:T(8,128)S(1)}, f32[2,32,1024]{2,1,0:T(8,128)S(1)}, u32[]{:S(2)}, u32[]{:S(2)}) %collective-permute-start.1) | collective-permute-done | bytes 262176 | tf_op jit(solution)/shard_map/ppermute | solution.py:356
  61.5 1.6 %copy-done.2 = bf16[1024,1024]{1,0:T(8,128)(2,1)S(1)} copy-done((bf16[1024,1024]{1,0:T(8,128)(2,1)S(1)}, bf16[1024,1024]{1,0:T(8,128)(2,1)}, u32[]{:S(2)}) %copy-start.2) | copy-done | bytes 2097176
  63.1 3.6 %first.1.bv_ref = f32[272,32,1024]{2,1,0:T(8,128)} custom-call(bf16[1024,1024]{1,0:T(8,128)(2,1)S(1)} %copy-done.1, bf16[1024,1024]{1,0:T(8,128)(2,1)S(1)} %copy-done.2, f32[8,1024]{1,0:T(8,128)S(1)} %copy-done.7, f32[6,8]{1,0:T(8,128)S(1)} %copy-done.8, f32[8,32,1024]{2,1,0:T(8,128)S(1)} %copy-done, f32[2,32,1024]{2,1,0:T(8,128)S(1)} %collective-permute-done.below_ref, ...), custom_call_target="tpu_custom_call" | custom-call | flops 1610612736 | bytes 7340032 | tf_op jit(solution)/shard_map/first/pallas_call | solution.py:237
  66.7 4.0 %second.3 = f32[1024,256]{1,0:T(8,128)S(1)} custom-call(bf16[17,1024,1024]{2,1,0:T(8,128)(2,1)} %get-tuple-element.17.both_ref, f32[8704,1024]{1,0:T(8,128)} %get-tuple-element.18.exits_ref, f32[1024,256]{1,0:T(8,128)} %second.2.mass_ref), custom_call_target="tpu_custom_call" | custom-call | flops 1610612736 | bytes 6291456 | tf_op jit(solution)/shard_map/second/pallas_call | solution.py:183
  70.7 1.0 copy-done.4
  71.7 10.3 %all-to-all-done.1.w_ref = f32[32,32,256]{2,1,0:T(8,128)} async-done(((f32[32,32,256]{2,1,0:T(8,128)}), f32[32,32,256]{2,1,0:T(8,128)}, u32[]{:S(2)}, u32[]{:S(2)}) %all-to-all-start.1) | async-done | bytes 1048608 | tf_op jit(solution)/shard_map/all_to_all | solution.py:350
  82.0 5.6 %all-to-all-start.2 = ((f32[32,32,256]{2,1,0:T(8,128)}), f32[32,32,256]{2,1,0:T(8,128)}, u32[]{:S(2)}, u32[]{:S(2)}) async-start(f32[32,32,256]{2,1,0:T(8,128)} %bitcast.8), calls=%async_computation.2 | async-start | bytes 2097152 | tf_op jit(solution)/shard_map/all_to_all | solution.py:350
  87.6 1.8 %once.1 = (f32[8,32,1024]{2,1,0:T(8,128)S(1)}, f32[2,32,1024]{2,1,0:T(8,128)S(1)}, f32[2,32,1024]{2,1,0:T(8,128)S(1)}) custom-call(f32[272,32,1024]{2,1,0:T(8,128)} %first.1.bv_ref, f32[32,32,256]{2,1,0:T(8,128)} %all-to-all-done.1.w_ref), custom_call_target="tpu_custom_call" | custom-call | flops 1048576 | bytes 4194304 | tf_op jit(solution)/shard_map/once/pallas_call | solution.py:267
  89.5 1.3 %collective-permute-start.2 = (f32[2,32,1024]{2,1,0:T(8,128)S(1)}, f32[2,32,1024]{2,1,0:T(8,128)S(1)}, u32[]{:S(2)}, u32[]{:S(2)}) collective-permute-start(f32[2,32,1024]{2,1,0:T(8,128)S(1)} %get-tuple-element.21), channel_id=1, source_target_pairs={{0,32},{32,64},{64,96},{96,128},{128,160},{160,192},{192,224},{1,3... | collective-permute-start | bytes 786440 | tf_op jit(solution)/shard_map/ppermute | solution.py:355
  90.8 1.3 %collective-permute-start.3 = (f32[2,32,1024]{2,1,0:T(8,128)S(1)}, f32[2,32,1024]{2,1,0:T(8,128)S(1)}, u32[]{:S(2)}, u32[]{:S(2)}) collective-permute-start(f32[2,32,1024]{2,1,0:T(8,128)S(1)} %get-tuple-element.22), channel_id=1, source_target_pairs={{32,0},{64,32},{96,64},{128,96},{160,128},{192,160},{224,192},{33,... | collective-permute-start | bytes 786440 | tf_op jit(solution)/shard_map/ppermute | solution.py:356
  92.1 3.8 %collective-permute-done.3.above_ref = f32[2,32,1024]{2,1,0:T(8,128)S(1)} collective-permute-done((f32[2,32,1024]{2,1,0:T(8,128)S(1)}, f32[2,32,1024]{2,1,0:T(8,128)S(1)}, u32[]{:S(2)}, u32[]{:S(2)}) %collective-permute-start.3) | collective-permute-done | bytes 262176 | tf_op jit(solution)/shard_map/ppermute | solution.py:356
  95.9 4.8 %twice.1.both_ref = f32[34,8,32,1024]{3,2,1,0:T(8,128)} custom-call(bf16[1024,1024]{1,0:T(8,128)(2,1)S(1)} %copy-done.1, bf16[1024,1024]{1,0:T(8,128)(2,1)S(1)} %copy-done.3, f32[8,1024]{1,0:T(8,128)S(1)} %copy-done.7, f32[6,8]{1,0:T(8,128)S(1)} %copy-done.8, f32[8,32,1024]{2,1,0:T(8,128)S(1)} %copy-done, f32[272,32,1024]{2,1,0:T(8,128)} %first.1.bv_ref, ...), custom_call_target="tpu_custom_call" | custom-call | flops 1610612736 | bytes 9437184 | tf_op jit(solution)/shard_map/twice/pallas_call | solution.py:304
  100.7 14.2 %all-to-all-done.2.w_ref = f32[32,32,256]{2,1,0:T(8,128)} async-done(((f32[32,32,256]{2,1,0:T(8,128)}), f32[32,32,256]{2,1,0:T(8,128)}, u32[]{:S(2)}, u32[]{:S(2)}) %all-to-all-start.2) | async-done | bytes 1048608 | tf_op jit(solution)/shard_map/all_to_all | solution.py:350
  115.0 2.9 %finish.1 = (f32[8,32,1024]{2,1,0:T(8,128)}, f32[8,32,1024]{2,1,0:T(8,128)}) custom-call(f32[34,8,32,1024]{3,2,1,0:T(8,128)} %twice.1.both_ref, f32[32,32,256]{2,1,0:T(8,128)} %all-to-all-done.2.w_ref), custom_call_target="tpu_custom_call" | custom-call | flops 1048576 | bytes 5242880 | tf_op jit(solution)/shard_map/finish/pallas_call | solution.py:331
  (17 shorter events, 0.1 us)
Async XLA Ops:
  2.7 39.8 %all-to-all-start = ((f32[32,32,256]{2,1,0:T(8,128)}), f32[32,32,256]{2,1,0:T(8,128)S(1)}, u32[]{:S(2)}, u32[]{:S(2)}) async-start(f32[32,32,256]{2,1,0:T(8,128)} %bitcast.11), calls=%async_computation | async-start | bytes 2097152 | tf_op jit(solution)/shard_map/all_to_all | solution.py:350
  42.5 1.0 copy-start.5
  43.4 1.2 %copy-start.6 = (f32[32,32,256]{2,1,0:T(8,128)S(1)}, f32[32,32,256]{2,1,0:T(8,128)}, u32[]{:S(2)}) copy-start(f32[32,32,256]{2,1,0:T(8,128)} %copy-done.5) | copy-start | bytes 3145732
  44.6 10.3 %copy-start = (f32[8,32,1024]{2,1,0:T(8,128)S(1)}, f32[8,32,1024]{2,1,0:T(8,128)}, u32[]{:S(2)}) copy-start(f32[8,32,1024]{2,1,0:T(8,128)} %v_ref.5) | copy-start | bytes 3145732
  44.7 16.8 %copy-start.1 = (bf16[1024,1024]{1,0:T(8,128)(2,1)S(1)}, bf16[1024,1024]{1,0:T(8,128)(2,1)}, u32[]{:S(2)}) copy-start(bf16[1024,1024]{1,0:T(8,128)(2,1)} %get-tuple-element.13.high_ref) | copy-start | bytes 6291460
  44.7 16.8 %copy-start.7 = (f32[8,1024]{1,0:T(8,128)S(1)}, f32[8,1024]{1,0:T(8,128)}, u32[]{:S(2)}) copy-start(f32[8,1024]{1,0:T(8,128)} %get-tuple-element.15.exits_ref) | copy-start | bytes 98308
  44.7 16.8 %copy-start.8 = (f32[6,8]{1,0:T(8,128)S(1)}, f32[6,8]{1,0:T(8,128)}, u32[]{:S(2)}) copy-start(f32[6,8]{1,0:T(8,128)} %get-tuple-element.16.coef_ref) | copy-start | bytes 580
  49.3 32.7 %all-to-all-start.1 = ((f32[32,32,256]{2,1,0:T(8,128)}), f32[32,32,256]{2,1,0:T(8,128)}, u32[]{:S(2)}, u32[]{:S(2)}) async-start(f32[32,32,256]{2,1,0:T(8,128)} %bitcast.6), calls=%async_computation.1 | async-start | bytes 2097152 | tf_op jit(solution)/shard_map/all_to_all | solution.py:350
  55.0 2.6 %collective-permute-start = (f32[2,32,1024]{2,1,0:T(8,128)S(1)}, f32[2,32,1024]{2,1,0:T(8,128)S(1)}, u32[]{:S(2)}, u32[]{:S(2)}) collective-permute-start(f32[2,32,1024]{2,1,0:T(8,128)S(1)} %get-tuple-element.25), channel_id=1, source_target_pairs={{0,32},{32,64},{64,96},{96,128},{128,160},{160,192},{192,224},{1,3... | collective-permute-start | bytes 786440 | tf_op jit(solution)/shard_map/ppermute | solution.py:355
  56.3 5.1 %collective-permute-start.1 = (f32[2,32,1024]{2,1,0:T(8,128)S(1)}, f32[2,32,1024]{2,1,0:T(8,128)S(1)}, u32[]{:S(2)}, u32[]{:S(2)}) collective-permute-start(f32[2,32,1024]{2,1,0:T(8,128)S(1)} %get-tuple-element.24), channel_id=1, source_target_pairs={{32,0},{64,32},{96,64},{128,96},{160,128},{192,160},{224,192},{33,... | collective-permute-start | bytes 786440 | tf_op jit(solution)/shard_map/ppermute | solution.py:356
  61.5 1.6 %copy-start.2 = (bf16[1024,1024]{1,0:T(8,128)(2,1)S(1)}, bf16[1024,1024]{1,0:T(8,128)(2,1)}, u32[]{:S(2)}) copy-start(bf16[1024,1024]{1,0:T(8,128)(2,1)} %get-tuple-element.14.low_ref) | copy-start | bytes 6291460
  70.7 1.0 copy-start.4
  82.0 33.0 %all-to-all-start.2 = ((f32[32,32,256]{2,1,0:T(8,128)}), f32[32,32,256]{2,1,0:T(8,128)}, u32[]{:S(2)}, u32[]{:S(2)}) async-start(f32[32,32,256]{2,1,0:T(8,128)} %bitcast.8), calls=%async_computation.2 | async-start | bytes 2097152 | tf_op jit(solution)/shard_map/all_to_all | solution.py:350
  87.6 8.3 %copy-start.3 = (bf16[1024,1024]{1,0:T(8,128)(2,1)S(1)}, bf16[1024,1024]{1,0:T(8,128)(2,1)}, u32[]{:S(2)}) copy-start(bf16[1024,1024]{1,0:T(8,128)(2,1)} %get-tuple-element.14.low_ref) | copy-start | bytes 6291460
  89.5 2.6 %collective-permute-start.2 = (f32[2,32,1024]{2,1,0:T(8,128)S(1)}, f32[2,32,1024]{2,1,0:T(8,128)S(1)}, u32[]{:S(2)}, u32[]{:S(2)}) collective-permute-start(f32[2,32,1024]{2,1,0:T(8,128)S(1)} %get-tuple-element.21), channel_id=1, source_target_pairs={{0,32},{32,64},{64,96},{96,128},{128,160},{160,192},{192,224},{1,3... | collective-permute-start | bytes 786440 | tf_op jit(solution)/shard_map/ppermute | solution.py:355
  90.8 5.1 %collective-permute-start.3 = (f32[2,32,1024]{2,1,0:T(8,128)S(1)}, f32[2,32,1024]{2,1,0:T(8,128)S(1)}, u32[]{:S(2)}, u32[]{:S(2)}) collective-permute-start(f32[2,32,1024]{2,1,0:T(8,128)S(1)} %get-tuple-element.22), channel_id=1, source_target_pairs={{32,0},{64,32},{96,64},{128,96},{160,128},{192,160},{224,192},{33,... | collective-permute-start | bytes 786440 | tf_op jit(solution)/shard_map/ppermute | solution.py:356

commit v6 on v4

--- a/solution.py
+++ b/solution.py
@@ -317,10 +317,11 @@
 def finish_kernel(step_ref, trans_ref, w_ref, out_t_ref, out_s_ref):
     levels, _, order = out_s_ref.shape
     parts = order // LANES
+    at = pl.program_id(0) * levels * parts
     for m in range(levels):
         for p in range(parts):
             cols = pl.ds(p * LANES, LANES)
-            more = w_ref[m * parts + p]
+            more = w_ref[at + m * parts + p]
             out_s_ref[m, :, cols] = step_ref[0, m, :, cols] + more
             out_t_ref[m, :, cols] = trans_ref[0, m, :, cols] + 0.2 * more
 
@@ -335,7 +336,7 @@
         in_specs=[
             pl.BlockSpec((1, tall, rows, order), lambda i: (0, i, 0, 0)),
             pl.BlockSpec((1, tall, rows, order), lambda i: (1, i, 0, 0)),
-            pl.BlockSpec((tall * (order // LANES), rows, LANES), lambda i: (i, 0, 0)),
+            WHOLE,
         ],
         out_specs=[block, block],
         out_shape=[shape, shape],

time: 115 us -> 115 us (level)
  no operation moved by 1% of the time
where the time goes in v6:
time: 115 us
  waiting for transfers between devices  49.9 us (43%)
  Pallas kernels  33.8 us (29%)
  starting transfers between devices  28.1 us (24%)
  local copies, waits for them, and re-layouts  2.07 us (2%)
    all_to_all x3, waiting for transfers between devices, swap(): lax.all_to_all(chunks, 'comp', split_axis=0, concat_axis=0, axis_index_gr...  46.1 us
    all_to_all x3, starting transfers between devices, swap(): lax.all_to_all(chunks, 'comp', split_axis=0, concat_axis=0, axis_index_gr...  22.9 us
    pallas_call x1, Pallas kernels, prepare(): pl.pallas_call(prepare_kernel, grid=(order // tall,), in_specs=[SCALARS,...  9.58 us
    pallas_call x2, Pallas kernels, turned(): pl.pallas_call(turned_kernel, grid=(order // tall,), in_specs=[pl.BlockSp...  8.95 us
    pallas_call x1, Pallas kernels, twice(): pl.pallas_call(twice_kernel, grid=(1,), in_specs=[WHOLE, WHOLE, WHOLE, SC...  4.89 us
    ppermute x2, waiting for transfers between devices, neighbours(): above = lax.ppermute(low, 'ctr', [(i + 1, i) for i in range(count - 1)])  3.83 us
    pallas_call x1, Pallas kernels, first(): pl.pallas_call(first_kernel, grid=(1,), in_specs=[WHOLE, WHOLE, WHOLE, SC...  3.61 us
    pallas_call x1, Pallas kernels, finish(): pl.pallas_call(finish_kernel, grid=(levels // tall,), in_specs=[pl.BlockS...  2.95 us
  transfers between devices with their start and end apart: 7, of which 4 were waited for; matrix products, arithmetic and copies ran while one was open for 1% of the time, Pallas kernels for 21%

profile of v6, /device:TPU:8, one launch (start us, length us, event | category | flops | bytes accessed | tf_op | source)
XLA Modules:
  0.0 114.8 jit_solution(4172759739496749823)
XLA Ops:
  0.6 2.1 %pack.1 = f32[8,4,32,256]{3,2,1,0:T(8,128)} custom-call(f32[8,32,1024]{2,1,0:T(8,128)} %v_ref.5), custom_call_target="tpu_custom_call" | custom-call | bytes 2097152 | tf_op jit(solution)/shard_map/pack/pallas_call | solution.py:156
  2.7 11.7 %all-to-all-start = ((f32[32,32,256]{2,1,0:T(8,128)}), f32[32,32,256]{2,1,0:T(8,128)S(1)}, u32[]{:S(2)}, u32[]{:S(2)}) async-start(f32[32,32,256]{2,1,0:T(8,128)} %bitcast.11), calls=%async_computation | async-start | bytes 2097152 | tf_op jit(solution)/shard_map/all_to_all | solution.py:353
  14.4 1.1 fusion
  15.5 1.3 %collective-permute-start = (f32[2,32,1024]{2,1,0:T(8,128)S(1)}, f32[2,32,1024]{2,1,0:T(8,128)S(1)}, u32[]{:S(2)}, u32[]{:S(2)}) collective-permute-start(f32[2,32,1024]{2,1,0:T(8,128)S(1)} %get-tuple-element.31), channel_id=1, source_target_pairs={{0,32},{32,64},{64,96},{96,128},{128,160},{160,192},{192,224},{1,3... | collective-permute-start | bytes 786440 | tf_op jit(solution)/shard_map/ppermute | solution.py:358
  16.8 1.3 %collective-permute-start.1 = (f32[2,32,1024]{2,1,0:T(8,128)S(1)}, f32[2,32,1024]{2,1,0:T(8,128)S(1)}, u32[]{:S(2)}, u32[]{:S(2)}) collective-permute-start(f32[2,32,1024]{2,1,0:T(8,128)S(1)} %get-tuple-element.30), channel_id=1, source_target_pairs={{32,0},{64,32},{96,64},{128,96},{160,128},{192,160},{224,192},{33,... | collective-permute-start | bytes 786440 | tf_op jit(solution)/shard_map/ppermute | solution.py:359
  18.1 9.6 %prepare.1 = (bf16[1024,1024]{1,0:T(8,128)(2,1)}, bf16[1024,1024]{1,0:T(8,128)(2,1)}, f32[8,1024]{1,0:T(8,128)}, bf16[17,1024,1024]{2,1,0:T(8,128)(2,1)}, f32[8704,1024]{1,0:T(8,128)}, /*index=5*/f32[6,8]{1,0:T(8,128)}) custom-call(f32[64]{0:T(128)} %rate_ref.1, s32[64]{0:T(128)} %code_ref.1, s32[1]{0:T(128)} %bitcast.start_ref, f32[1,64]{1,0:T(1,128)} %bitcast.12, ...), custom_call_target="tpu_custom_call" | custom-call | flops 134217728 | bytes 16777216 | tf_op jit(solution)/shard_map/prepare/pallas_call | solution.py:125
  27.7 0.0 collective-permute-done.below_ref
  27.7 14.8 %all-to-all-done = f32[32,32,256]{2,1,0:T(8,128)S(1)} async-done(((f32[32,32,256]{2,1,0:T(8,128)}), f32[32,32,256]{2,1,0:T(8,128)S(1)}, u32[]{:S(2)}, u32[]{:S(2)}) %all-to-all-start) | async-done | bytes 1048608 | tf_op jit(solution)/shard_map/all_to_all | solution.py:353
  42.5 4.5 %second.2.mass_ref = f32[1024,256]{1,0:T(8,128)} custom-call(bf16[17,1024,1024]{2,1,0:T(8,128)(2,1)} %get-tuple-element.20.high_ref.low_ref, bf16[17,1024,1024]{2,1,0:T(8,128)(2,1)} %get-tuple-element.20.high_ref.low_ref, f32[8704,1024]{1,0:T(8,128)} %get-tuple-element.21.exits_ref, f32[1024,256]{1,0:T(8,128)S(1)} %bitcast.8), custom_call_target="tpu_custom_call" | custom-call | flops 1610612736 | bytes 6291456 | tf_op jit(solution)/shard_map/second/pallas_call | solution.py:183
  46.9 5.6 %all-to-all-start.1 = ((f32[32,32,256]{2,1,0:T(8,128)}), f32[32,32,256]{2,1,0:T(8,128)}, u32[]{:S(2)}, u32[]{:S(2)}) async-start(f32[32,32,256]{2,1,0:T(8,128)} %bitcast.6), calls=%async_computation.1 | async-start | bytes 2097152 | tf_op jit(solution)/shard_map/all_to_all | solution.py:353
  52.5 0.0 copy-start
  52.6 4.5 %second.3 = f32[1024,256]{1,0:T(8,128)S(1)} custom-call(bf16[17,1024,1024]{2,1,0:T(8,128)(2,1)} %get-tuple-element.20.high_ref.low_ref, bf16[17,1024,1024]{2,1,0:T(8,128)(2,1)} %get-tuple-element.20.high_ref.low_ref, f32[8704,1024]{1,0:T(8,128)} %get-tuple-element.21.exits_ref, f32[1024,256]{1,0:T(8,128)} %second.2.mass_ref), custom_call_target="tpu_custom_call" | custom-call | flops 1610612736 | bytes 6291456 | tf_op jit(solution)/shard_map/second/pallas_call | solution.py:183
  57.1 0.0 copy-start.4
  57.1 1.0 copy-done.4
  58.1 3.6 %first.1.bv_ref = f32[272,32,1024]{2,1,0:T(8,128)} custom-call(bf16[1024,1024]{1,0:T(8,128)(2,1)S(1)} %copy-done.1, bf16[1024,1024]{1,0:T(8,128)(2,1)S(1)} %copy-done.2, f32[8,1024]{1,0:T(8,128)S(1)} %copy-done.7, f32[6,8]{1,0:T(8,128)S(1)} %copy-done.8, f32[8,32,1024]{2,1,0:T(8,128)S(1)} %copy-done, f32[2,32,1024]{2,1,0:T(8,128)S(1)} %collective-permute-done.below_ref, ...), custom_call_target="tpu_custom_call" | custom-call | flops 1610612736 | bytes 7340032 | tf_op jit(solution)/shard_map/first/pallas_call | solution.py:238
  61.7 17.9 %all-to-all-done.1.w_ref = f32[32,32,256]{2,1,0:T(8,128)} async-done(((f32[32,32,256]{2,1,0:T(8,128)}), f32[32,32,256]{2,1,0:T(8,128)}, u32[]{:S(2)}, u32[]{:S(2)}) %all-to-all-start.1) | async-done | bytes 1048608 | tf_op jit(solution)/shard_map/all_to_all | solution.py:353
  79.6 5.6 %all-to-all-start.2 = ((f32[32,32,256]{2,1,0:T(8,128)}), f32[32,32,256]{2,1,0:T(8,128)}, u32[]{:S(2)}, u32[]{:S(2)}) async-start(f32[32,32,256]{2,1,0:T(8,128)} %bitcast.9), calls=%async_computation.2 | async-start | bytes 2097152 | tf_op jit(solution)/shard_map/all_to_all | solution.py:353
  85.2 1.8 %once.1 = (f32[8,32,1024]{2,1,0:T(8,128)S(1)}, f32[2,32,1024]{2,1,0:T(8,128)S(1)}, f32[2,32,1024]{2,1,0:T(8,128)S(1)}) custom-call(f32[272,32,1024]{2,1,0:T(8,128)} %first.1.bv_ref, f32[32,32,256]{2,1,0:T(8,128)} %all-to-all-done.1.w_ref), custom_call_target="tpu_custom_call" | custom-call | flops 1048576 | bytes 4194304 | tf_op jit(solution)/shard_map/once/pallas_call | solution.py:268
  87.1 1.3 %collective-permute-start.2 = (f32[2,32,1024]{2,1,0:T(8,128)S(1)}, f32[2,32,1024]{2,1,0:T(8,128)S(1)}, u32[]{:S(2)}, u32[]{:S(2)}) collective-permute-start(f32[2,32,1024]{2,1,0:T(8,128)S(1)} %get-tuple-element.27), channel_id=1, source_target_pairs={{0,32},{32,64},{64,96},{96,128},{128,160},{160,192},{192,224},{1,3... | collective-permute-start | bytes 786440 | tf_op jit(solution)/shard_map/ppermute | solution.py:358
  88.4 1.3 %collective-permute-start.3 = (f32[2,32,1024]{2,1,0:T(8,128)S(1)}, f32[2,32,1024]{2,1,0:T(8,128)S(1)}, u32[]{:S(2)}, u32[]{:S(2)}) collective-permute-start(f32[2,32,1024]{2,1,0:T(8,128)S(1)} %get-tuple-element.28), channel_id=1, source_target_pairs={{32,0},{64,32},{96,64},{128,96},{160,128},{192,160},{224,192},{33,... | collective-permute-start | bytes 786440 | tf_op jit(solution)/shard_map/ppermute | solution.py:359
  89.7 3.8 %collective-permute-done.3.above_ref = f32[2,32,1024]{2,1,0:T(8,128)S(1)} collective-permute-done((f32[2,32,1024]{2,1,0:T(8,128)S(1)}, f32[2,32,1024]{2,1,0:T(8,128)S(1)}, u32[]{:S(2)}, u32[]{:S(2)}) %collective-permute-start.3) | collective-permute-done | bytes 262176 | tf_op jit(solution)/shard_map/ppermute | solution.py:359
  93.5 4.9 %twice.1.step_ref.trans_ref = f32[34,8,32,1024]{3,2,1,0:T(8,128)} custom-call(bf16[1024,1024]{1,0:T(8,128)(2,1)S(1)} %copy-done.1, bf16[1024,1024]{1,0:T(8,128)(2,1)S(1)} %copy-done.3, f32[8,1024]{1,0:T(8,128)S(1)} %copy-done.7, f32[6,8]{1,0:T(8,128)S(1)} %copy-done.8, f32[8,32,1024]{2,1,0:T(8,128)S(1)} %copy-done, f32[272,32,1024]{2,1,0:T(8,128)} %first.1.bv_ref, ...), custom_call_target="tpu_custom_call" | custom-call | flops 1610612736 | bytes 9437184 | tf_op jit(solution)/shard_map/twice/pallas_call | solution.py:305
  98.4 13.4 %all-to-all-done.2.w_ref = f32[32,32,256]{2,1,0:T(8,128)} async-done(((f32[32,32,256]{2,1,0:T(8,128)}), f32[32,32,256]{2,1,0:T(8,128)}, u32[]{:S(2)}, u32[]{:S(2)}) %all-to-all-start.2) | async-done | bytes 1048608 | tf_op jit(solution)/shard_map/all_to_all | solution.py:353
  111.8 2.9 %finish.1 = (f32[8,32,1024]{2,1,0:T(8,128)}, f32[8,32,1024]{2,1,0:T(8,128)}) custom-call(f32[34,8,32,1024]{3,2,1,0:T(8,128)} %twice.1.step_ref.trans_ref, f32[34,8,32,1024]{3,2,1,0:T(8,128)} %twice.1.step_ref.trans_ref, f32[32,32,256]{2,1,0:T(8,128)} %all-to-all-done.2.w_ref), custom_call_target="tpu_custom_call" | custom-call | flops 1048576 | bytes 5242880 | tf_op jit(solution)/shard_map/finish/pallas_call | solution.py:333
  (17 shorter events, 0.0 us)
Async XLA Ops:
  2.7 39.8 %all-to-all-start = ((f32[32,32,256]{2,1,0:T(8,128)}), f32[32,32,256]{2,1,0:T(8,128)S(1)}, u32[]{:S(2)}, u32[]{:S(2)}) async-start(f32[32,32,256]{2,1,0:T(8,128)} %bitcast.11), calls=%async_computation | async-start | bytes 2097152 | tf_op jit(solution)/shard_map/all_to_all | solution.py:353
  15.5 12.2 %collective-permute-start = (f32[2,32,1024]{2,1,0:T(8,128)S(1)}, f32[2,32,1024]{2,1,0:T(8,128)S(1)}, u32[]{:S(2)}, u32[]{:S(2)}) collective-permute-start(f32[2,32,1024]{2,1,0:T(8,128)S(1)} %get-tuple-element.31), channel_id=1, source_target_pairs={{0,32},{32,64},{64,96},{96,128},{128,160},{160,192},{192,224},{1,3... | collective-permute-start | bytes 786440 | tf_op jit(solution)/shard_map/ppermute | solution.py:358
  16.8 10.9 %collective-permute-start.1 = (f32[2,32,1024]{2,1,0:T(8,128)S(1)}, f32[2,32,1024]{2,1,0:T(8,128)S(1)}, u32[]{:S(2)}, u32[]{:S(2)}) collective-permute-start(f32[2,32,1024]{2,1,0:T(8,128)S(1)} %get-tuple-element.30), channel_id=1, source_target_pairs={{32,0},{64,32},{96,64},{128,96},{160,128},{192,160},{224,192},{33,... | collective-permute-start | bytes 786440 | tf_op jit(solution)/shard_map/ppermute | solution.py:359
  27.7 19.2 %copy-start.5 = (f32[2,32,1024]{2,1,0:T(8,128)}, f32[2,32,1024]{2,1,0:T(8,128)S(1)}, u32[]{:S(2)}) copy-start(f32[2,32,1024]{2,1,0:T(8,128)S(1)} %collective-permute-done.1.above_ref) | copy-start | bytes 786436
  46.9 32.7 %all-to-all-start.1 = ((f32[32,32,256]{2,1,0:T(8,128)}), f32[32,32,256]{2,1,0:T(8,128)}, u32[]{:S(2)}, u32[]{:S(2)}) async-start(f32[32,32,256]{2,1,0:T(8,128)} %bitcast.6), calls=%async_computation.1 | async-start | bytes 2097152 | tf_op jit(solution)/shard_map/all_to_all | solution.py:353
  52.5 5.5 %copy-start = (f32[8,32,1024]{2,1,0:T(8,128)S(1)}, f32[8,32,1024]{2,1,0:T(8,128)}, u32[]{:S(2)}) copy-start(f32[8,32,1024]{2,1,0:T(8,128)} %v_ref.5) | copy-start | bytes 3145732
  52.6 5.5 %copy-start.1 = (bf16[1024,1024]{1,0:T(8,128)(2,1)S(1)}, bf16[1024,1024]{1,0:T(8,128)(2,1)}, u32[]{:S(2)}) copy-start(bf16[1024,1024]{1,0:T(8,128)(2,1)} %get-tuple-element.16.high_ref) | copy-start | bytes 6291460
  52.6 5.5 %copy-start.2 = (bf16[1024,1024]{1,0:T(8,128)(2,1)S(1)}, bf16[1024,1024]{1,0:T(8,128)(2,1)}, u32[]{:S(2)}) copy-start(bf16[1024,1024]{1,0:T(8,128)(2,1)} %get-tuple-element.17.low_ref) | copy-start | bytes 6291460
  52.6 5.5 %copy-start.6 = (f32[2,32,1024]{2,1,0:T(8,128)S(1)}, f32[2,32,1024]{2,1,0:T(8,128)}, u32[]{:S(2)}) copy-start(f32[2,32,1024]{2,1,0:T(8,128)} %copy-done.5) | copy-start | bytes 786436
  52.6 5.5 %copy-start.7 = (f32[8,1024]{1,0:T(8,128)S(1)}, f32[8,1024]{1,0:T(8,128)}, u32[]{:S(2)}) copy-start(f32[8,1024]{1,0:T(8,128)} %get-tuple-element.18.exits_ref) | copy-start | bytes 98308
  52.6 5.5 %copy-start.8 = (f32[6,8]{1,0:T(8,128)S(1)}, f32[6,8]{1,0:T(8,128)}, u32[]{:S(2)}) copy-start(f32[6,8]{1,0:T(8,128)} %get-tuple-element.19.coef_ref) | copy-start | bytes 580
  57.1 1.0 copy-start.4
  79.6 32.2 %all-to-all-start.2 = ((f32[32,32,256]{2,1,0:T(8,128)}), f32[32,32,256]{2,1,0:T(8,128)}, u32[]{:S(2)}, u32[]{:S(2)}) async-start(f32[32,32,256]{2,1,0:T(8,128)} %bitcast.9), calls=%async_computation.2 | async-start | bytes 2097152 | tf_op jit(solution)/shard_map/all_to_all | solution.py:353
  85.2 8.3 %copy-start.3 = (bf16[1024,1024]{1,0:T(8,128)(2,1)S(1)}, bf16[1024,1024]{1,0:T(8,128)(2,1)}, u32[]{:S(2)}) copy-start(bf16[1024,1024]{1,0:T(8,128)(2,1)} %get-tuple-element.17.low_ref) | copy-start | bytes 6291460
  87.1 2.6 %collective-permute-start.2 = (f32[2,32,1024]{2,1,0:T(8,128)S(1)}, f32[2,32,1024]{2,1,0:T(8,128)S(1)}, u32[]{:S(2)}, u32[]{:S(2)}) collective-permute-start(f32[2,32,1024]{2,1,0:T(8,128)S(1)} %get-tuple-element.27), channel_id=1, source_target_pairs={{0,32},{32,64},{64,96},{96,128},{128,160},{160,192},{192,224},{1,3... | collective-permute-start | bytes 786440 | tf_op jit(solution)/shard_map/ppermute | solution.py:358
  88.4 5.1 %collective-permute-start.3 = (f32[2,32,1024]{2,1,0:T(8,128)S(1)}, f32[2,32,1024]{2,1,0:T(8,128)S(1)}, u32[]{:S(2)}, u32[]{:S(2)}) collective-permute-start(f32[2,32,1024]{2,1,0:T(8,128)S(1)} %get-tuple-element.28), channel_id=1, source_target_pairs={{32,0},{64,32},{96,64},{128,96},{160,128},{192,160},{224,192},{33,... | collective-permute-start | bytes 786440 | tf_op jit(solution)/shard_map/ppermute | solution.py:359
